TPU v7x, 512 devices: a whole 4x8x8 slice. The times are simulated.
512 devices in a mesh: wide: 128 (over y, z, core), narrow: 4 (over x).
Axes of the slice: x: 4, y: 8, z: 8, core: 2. Of those that a mesh axis runs over, the one named last changes fastest.
Arguments:
- tokens: bfloat16 [65536, 2048], P(('wide', 'narrow')), may hold values from -6 to 6
- route_slot: int32 [65536, 2], P(('wide', 'narrow')), may hold values from 0 to 2, all different within a row
- route_code: int32 [65536, 2], P(('wide', 'narrow')), may hold values from 1 to 255
- group_hits: int32 [128, 3], replicated, may hold values from 0 to 127, as said below
- gate_w: bfloat16 [2048, 384, 128], P('wide', 'narrow'), may hold values from -0.125 to 0.125
- up_w: bfloat16 [2048, 384, 128], P('wide', 'narrow'), may hold values from -0.125 to 0.125
- down_w: bfloat16 [2048, 384, 128], P('wide', 'narrow'), may hold values from -0.3125 to 0.3125
- gate_scale: bfloat16 [2048, 128], P('wide'), may hold values from 0.5 to 2
- up_scale: bfloat16 [2048, 128], P('wide'), may hold values from 0.5 to 2
- down_scale: bfloat16 [2048, 128], P('wide'), may hold values from 0.5 to 2
- cotangent: bfloat16 [65536, 2048], P(('wide', 'narrow')), may hold values from -6 to 6
Outputs:
- mixed: bfloat16 [65536, 2048], P(('wide', 'narrow'))
- token_grad: bfloat16 [65536, 2048], P(('wide', 'narrow'))
- gate_grad: bfloat16 [2048, 384, 128], P('wide', 'narrow')
- up_grad: bfloat16 [2048, 384, 128], P('wide', 'narrow')
- down_grad: bfloat16 [2048, 384, 128], P('wide', 'narrow')
Inputs may be any that keep to these rules, and one draw needn't show every extreme that they name: `group_hits`: row g names 3 different experts, and every expert is named in exactly 3 rows. `route_slot`: each row names 2 different slots.
All inputs are finite; a program needn't handle non-finite values.
Results may differ from a plain program's by a relative error of at most 0.013.
Values may be sent and summed in bfloat16 or wider, within the bound.
No kernel may reach another device: no remote copies, remote signals or barrier semaphores. Data moves between devices by JAX's collectives and lax.ppermute only.
A program may use at most 128 MiB of HBM per device.

v0:
```python
import jax
import jax.numpy as jnp
from jax import lax
from jax.experimental import pallas as pl
from jax.experimental.pallas import tpu as pltpu
from jax.sharding import PartitionSpec as P

LANES = 128
VMEM_LIMIT = 56 * 1024 * 1024


def lane_index(shape):
    return lax.broadcasted_iota(jnp.int32, shape, len(shape) - 1)


def pack_kernel(hits_ref, gate_ref, up_ref, down_ref, gs_ref, us_ref, ds_ref, out_ref, held, wide):
    rows, block, experts = gate_ref.shape
    groups = out_ref.shape[0]
    for m, (w_ref, s_ref) in enumerate(((gate_ref, gs_ref), (up_ref, us_ref), (down_ref, ds_ref))):
        wide[...] = s_ref[...].astype(jnp.float32)

        @pl.loop(0, rows)
        def _(r, m=m, w_ref=w_ref):
            scale = wide[pl.ds(r, 1), :]
            scaled = w_ref[r].astype(jnp.float32) * scale
            scaled = scaled.astype(jnp.bfloat16).astype(jnp.float32)
            full = jnp.concatenate([scaled, jnp.zeros((LANES - block, experts), jnp.float32)], axis=0)
            start = pl.multiple_of((m * rows + r) * experts, experts)
            held[pl.ds(start, experts), :] = full.T

    lane = lane_index((rows, LANES))

    @pl.loop(0, groups, unroll=2)
    def _(g):
        tail = jnp.zeros((rows, LANES), jnp.float32)
        for m in range(3):
            part = [
                held[pl.ds(m * rows * experts + hits_ref[3 * g + k], rows, stride=experts), :]
                for k in range(3)
            ]
            second = pltpu.roll(part[1], 96, 1)
            third = pltpu.roll(part[2], 64, 1)
            out_ref[g, :, 256 * m : 256 * m + 128] = jnp.where(lane < 96, part[0], second).astype(jnp.bfloat16)
            out_ref[g, :, 256 * m + 128 : 256 * m + 256] = jnp.where(lane < 64, second, third).astype(jnp.bfloat16)
            ext = third if m == 0 else part[2] if m == 2 else pltpu.roll(part[2], 96, 1)
            tail = jnp.where((lane >= 32 * m) & (lane < 32 * m + 32), ext, tail)
        out_ref[g, :, 768:896] = tail.astype(jnp.bfloat16)


def settle_kernel(hits_ref, recv_ref, gate_ref, up_ref, down_ref, acc):
    rows, block, experts = gate_ref.shape
    groups = recv_ref.shape[0]
    acc[...] = jnp.zeros_like(acc)

    @pl.loop(0, groups)
    def _(g):
        spots = [hits_ref[3 * g + k] * rows for k in range(3)]
        tail = recv_ref[g, :, 768:896].astype(jnp.float32)
        lane = lane_index((rows, LANES))
        terms = []
        for m in range(3):
            low = recv_ref[g, :, 256 * m : 256 * m + 128].astype(jnp.float32)
            high = recv_ref[g, :, 256 * m + 128 : 256 * m + 256].astype(jnp.float32)
            second = pltpu.roll(jnp.where(lane < 64, high, low), 32, 1)
            third = pltpu.roll(high, 64, 1)
            ext = tail if m == 2 else pltpu.roll(tail, 64 - 32 * m, 1)
            third = jnp.where(lane < 64, third, ext)
            terms.append((low, second, third))
        old = [
            [acc[m, pl.ds(pl.multiple_of(spots[k], rows), rows), :] for k in range(3)] for m in range(3)
        ]
        for m in range(3):
            for k in range(3):
                acc[m, pl.ds(pl.multiple_of(spots[k], rows), rows), :] = old[m][k] + terms[m][k]

    for m, out_ref in enumerate((gate_ref, up_ref, down_ref)):

        @pl.loop(0, rows)
        def _(r, m=m, out_ref=out_ref):
            mine = acc[m, pl.ds(r, experts, stride=rows), :]
            out_ref[r] = mine.T[:block].astype(jnp.bfloat16)


def dot(left, right):
    return lax.dot_general(left, right, (((1,), (0,)), ((), ())), preferred_element_type=jnp.float32)


def dot_t(left, right):
    return lax.dot_general(left, right, (((1,), (1,)), ((), ())), preferred_element_type=jnp.float32)


def middle_kernel(x_ref, dy_ref, xt_ref, dyt_ref, rw_ref, w_ref, term_ref, act_ref):
    tok = x_ref.shape[0]
    width = x_ref.shape[1]
    chunk = 256

    @pl.loop(0, tok // chunk)
    def _(i):
        rows = pl.ds(pl.multiple_of(i * chunk, chunk), chunk)
        gate = dot(x_ref[rows, :], w_ref[:, 0:256])
        up = dot(x_ref[rows, :], w_ref[:, 256:512])
        back = dot(dy_ref[rows, :], w_ref[:, 512:768])
        tail_x = dot(x_ref[rows, :], w_ref[:, 768:896])
        tail_dy = dot(dy_ref[rows, :], w_ref[:, 768:896])
        rw = rw_ref[rows, :].astype(jnp.float32)
        lane = lane_index((chunk, 256))
        main_rw = jnp.where(lane < 96, rw[:, 0:1], jnp.where(lane < 192, rw[:, 1:2], rw[:, 2:3]))

        def finish(gate, up, back, share):
            sig = jax.nn.sigmoid(gate)
            silu = gate * sig
            weighted = share * silu * up
            d_act = share * back
            d_gate = d_act * up * sig * (1.0 + gate * (1.0 - sig))
            return d_gate, d_act * silu, weighted

        d_gate, d_up, weighted = finish(gate, up, back, main_rw)
        act_ref[rows, 0:256] = d_gate.astype(jnp.bfloat16)
        act_ref[rows, 256:512] = d_up.astype(jnp.bfloat16)
        act_ref[rows, 512:768] = weighted.astype(jnp.bfloat16)
        d_gate, d_up, weighted = finish(
            tail_x, pltpu.roll(tail_x, 96, 1), pltpu.roll(tail_dy, 64, 1), rw[:, 2:3]
        )
        lane = lane_index((chunk, LANES))
        from_x = jnp.where(lane < 32, d_gate, jnp.where(lane < 64, pltpu.roll(d_up, 32, 1), 0.0))
        from_dy = jnp.where((lane >= 64) & (lane < 96), pltpu.roll(weighted, 64, 1), 0.0)
        act_ref[rows, 768:896] = from_x.astype(jnp.bfloat16)
        act_ref[rows, 896:1024] = from_dy.astype(jnp.bfloat16)

    @pl.loop(0, width // 512)
    def _(i):
        cols = pl.ds(pl.multiple_of(i * 512, 512), 512)
        xt = xt_ref[cols, :]
        dyt = dyt_ref[cols, :]
        term_ref[cols, 0:256] = dot(xt, act_ref[:, 0:256]).astype(jnp.bfloat16)
        term_ref[cols, 256:512] = dot(xt, act_ref[:, 256:512]).astype(jnp.bfloat16)
        term_ref[cols, 512:768] = dot(dyt, act_ref[:, 512:768]).astype(jnp.bfloat16)
        tail = dot(xt, act_ref[:, 768:896]) + dot(dyt, act_ref[:, 896:1024])
        term_ref[cols, 768:896] = tail.astype(jnp.bfloat16)


def out_kernel(act_ref, w_ref, mixed_ref, grad_ref):
    width = w_ref.shape[0]

    @pl.loop(0, width // 512)
    def _(i):
        cols = pl.ds(pl.multiple_of(i * 512, 512), 512)
        tail = w_ref[cols, 768:896]
        mixed = dot_t(act_ref[:, 512:768], w_ref[cols, 512:768]) + dot_t(act_ref[:, 896:1024], tail)
        mixed_ref[:, cols] = mixed.astype(jnp.bfloat16)
        grad = dot_t(act_ref[:, 0:512], w_ref[cols, 0:512]) + dot_t(act_ref[:, 768:896], tail)
        grad_ref[:, cols] = grad.astype(jnp.bfloat16)


def flip_kernel(x_ref, dy_ref, xt_ref, dyt_ref):
    @pl.loop(0, x_ref.shape[1] // 512)
    def _(i):
        cols = pl.ds(pl.multiple_of(i * 512, 512), 512)
        xt_ref[cols, :] = x_ref[:, cols].T
        dyt_ref[cols, :] = dy_ref[:, cols].T


def vmem_call(body, out_shapes, inputs, scratch=(), smem=0, flops=0):
    inside = pl.BlockSpec(memory_space=pltpu.VMEM)
    scalar = pl.BlockSpec(memory_space=pltpu.SMEM)
    moved = sum(a.size * a.dtype.itemsize for a in (*inputs, *out_shapes))
    return pl.pallas_call(
        body,
        out_shape=out_shapes,
        in_specs=[scalar] * smem + [inside] * (len(inputs) - smem),
        out_specs=[inside] * len(out_shapes),
        scratch_shapes=list(scratch),
        compiler_params=pltpu.CompilerParams(vmem_limit_bytes=VMEM_LIMIT),
        cost_estimate=pl.CostEstimate(flops=flops, bytes_accessed=moved, transcendentals=0),
    )(*inputs)


def shape(*dims):
    return jax.ShapeDtypeStruct(dims, jnp.bfloat16)


def pack(hits, weights, scales):
    rows, _, experts = weights[0].shape
    held = pltpu.VMEM((3 * rows * experts, LANES), jnp.float32)
    wide = pltpu.VMEM((rows, experts), jnp.float32)
    return vmem_call(
        pack_kernel, [shape(hits.shape[0], rows, 896)], (hits.reshape(-1), *weights, *scales), (held, wide), 1
    )[0]


def settle(hits, received, like):
    rows, _, experts = like.shape
    acc = pltpu.VMEM((3, experts * rows, LANES), jnp.float32)
    return vmem_call(settle_kernel, [shape(*like.shape)] * 3, (hits.reshape(-1), received), (acc,), 1)


def per_device(
    tokens,
    route_slot,
    route_code,
    group_hits,
    gate_w,
    up_w,
    down_w,
    gate_scale,
    up_scale,
    down_scale,
    cotangent,
):
    hit_count = group_hits.shape[1]
    groups = group_hits.shape[0]
    owner_rows = gate_w.shape[0]
    codes = route_code.astype(jnp.float32)
    shares = codes / jnp.sum(codes, axis=1, keepdims=True)
    slots = jnp.arange(hit_count, dtype=jnp.int32)
    picked = (route_slot[:, :, None] == slots[None, None, :]).astype(jnp.float32)
    rweight = jnp.sum(picked * shares[:, :, None], axis=1).astype(jnp.bfloat16)
    sent = pack(group_hits, (gate_w, up_w, down_w), (gate_scale, up_scale, down_scale))
    received = lax.all_to_all(sent, "wide", split_axis=0, concat_axis=0, tiled=True)
    group_x = lax.all_gather(tokens, "narrow", axis=0, tiled=True)
    group_dy = lax.all_gather(cotangent, "narrow", axis=0, tiled=True)
    group_rw = lax.all_gather(rweight, "narrow", axis=0, tiled=True)
    tok, width = group_x.shape
    flipped = vmem_call(flip_kernel, [shape(width, tok)] * 2, (group_x, group_dy))
    weights = received.reshape(width, 896)
    terms, act = vmem_call(
        middle_kernel,
        [shape(width, 896), shape(tok, 1024)],
        (group_x, group_dy, *flipped, group_rw, weights),
        flops=2 * 6 * tok * width * 288,
    )
    back = lax.all_to_all(
        terms.reshape(groups, owner_rows, 896), "wide", split_axis=0, concat_axis=0, tiled=True
    )
    mixed, token_grad = vmem_call(
        out_kernel, [shape(tok, width)] * 2, (act, weights), flops=2 * 3 * tok * width * 288
    )
    mixed = lax.psum_scatter(mixed, "narrow", scatter_dimension=0, tiled=True)
    token_grad = lax.psum_scatter(token_grad, "narrow", scatter_dimension=0, tiled=True)
    gate_grad, up_grad, down_grad = settle(group_hits, back, gate_w)
    return (mixed, token_grad, gate_grad, up_grad, down_grad)


def solution(mesh):
    placed = (
        P(("wide", "narrow"), None),
        P(("wide", "narrow"), None),
        P(("wide", "narrow"), None),
        P(),
        P("wide", "narrow", None),
        P("wide", "narrow", None),
        P("wide", "narrow", None),
        P("wide", None),
        P("wide", None),
        P("wide", None),
        P(("wide", "narrow"), None),
    )
    return jax.shard_map(
        per_device,
        mesh=mesh,
        in_specs=placed,
        out_specs=(
            P(("wide", "narrow"), None),
            P(("wide", "narrow"), None),
            P("wide", "narrow", None),
            P("wide", "narrow", None),
            P("wide", "narrow", None),
        ),
        check_vma=False,
    )
```

profile of v0, /device:TPU:25, one launch (start us, length us, event | category | flops | bytes accessed | tf_op | source)
XLA Modules:
  0.0 277.1 jit_solution(14429349870124568808)
XLA Ops:
  7.2 0.8 copy.24
  8.0 0.8 reshape.23.hits_ref
  8.8 19.4 %shard_map.147 = bf16[128,16,896]{2,1,0:T(8,128)(2,1)} custom-call(s32[384]{0:T(512)} %reshape.23.hits_ref, bf16[16,96,128]{2,1,0:T(8,128)(2,1)} %gate_ref.1, bf16[16,96,128]{2,1,0:T(8,128)(2,1)} %up_ref.1, bf16[16,96,128]{2,1,0:T(8,128)(2,1)} %down_ref.1, bf16[16,128]{1,0:T(8,128)(2,1)} %gs_ref.1, bf16[16,128]{1,0:T(8,128)(2,1)} %us_ref.1, ...), custom_call_target="tpu_custom_call" | custom-call | bytes 4863488 | tf_op jit(solution)/shard_map/pallas_call | solution.py:167
  28.2 0.0 copy-start.1
  28.2 0.0 copy-start
  28.2 18.2 %all-to-all-start = ((bf16[128,16,896]{2,1,0:T(8,128)(2,1)}), bf16[128,16,896]{2,1,0:T(8,128)(2,1)}, u32[]{:S(2)}, u32[]{:S(2)}) async-start(bf16[128,16,896]{2,1,0:T(8,128)(2,1)} %shard_map.147), calls=%async_computation | async-start | bytes 7340032 | tf_op jit(solution)/shard_map/all_to_all | solution.py:219
  46.4 0.0 all-gather.3.cloned.1.call-start
  46.4 0.7 all-gather.3.cloned.1.call-update
  47.1 0.0 all-gather.5.cloned.1.call-start
  47.2 0.7 all-gather.5.cloned.1.call-update
  47.9 0.0 reduce-scatter.3.cloned.1.call-start
  47.9 0.0 copy-done.1
  48.0 0.0 copy-done
  48.0 0.1 copy.23
  48.1 11.1 %all_gather.11.rw_ref = bf16[512,3]{1,0:T(8,128)(2,1)} all-gather(bf16[128,3]{1,0:T(8,128)(2,1)S(1)} %copy.23), channel_id=1, replica_groups=mesh['wide'=128,'narrow'=4] {'narrow'}, dimensions={0}, use_global_device_ids=true | all-gather | bytes 3840 | tf_op jit(solution)/shard_map/all_gather | solution.py:222
  59.2 26.8 %all-gather.3.cloned.1.call-done.x_ref = bf16[512,2048]{1,0:T(8,128)(2,1)} async-done(((bf16[128,2048]{1,0:T(8,128)(2,1)}), bf16[512,2048]{1,0:T(8,128)(2,1)}) %all-gather.3.cloned.1.call-update) | async-done | bytes 2097168 | tf_op jit(solution)/shard_map/all_gather | solution.py:220
  86.0 38.4 %all-gather.5.cloned.1.call-done.dy_ref = bf16[512,2048]{1,0:T(8,128)(2,1)} async-done(((bf16[128,2048]{1,0:T(8,128)(2,1)}), bf16[512,2048]{1,0:T(8,128)(2,1)}) %all-gather.5.cloned.1.call-update) | async-done | bytes 2097168 | tf_op jit(solution)/shard_map/all_gather | solution.py:221
  124.3 5.4 %shard_map.146 = (bf16[2048,512]{1,0:T(8,128)(2,1)}, bf16[2048,512]{1,0:T(8,128)(2,1)}) custom-call(bf16[512,2048]{1,0:T(8,128)(2,1)} %all-gather.3.cloned.1.call-done.x_ref, bf16[512,2048]{1,0:T(8,128)(2,1)} %all-gather.5.cloned.1.call-done.dy_ref), custom_call_target="tpu_custom_call" | custom-call | bytes 8388608 | tf_op jit(solution)/shard_map/pallas_call | solution.py:167
  129.8 3.2 %all-to-all-done = bf16[128,16,896]{2,1,0:T(8,128)(2,1)} async-done(((bf16[128,16,896]{2,1,0:T(8,128)(2,1)}), bf16[128,16,896]{2,1,0:T(8,128)(2,1)}, u32[]{:S(2)}, u32[]{:S(2)}) %all-to-all-start) | async-done | bytes 3670048 | tf_op jit(solution)/shard_map/all_to_all | solution.py:219
  133.0 13.2 %shard_map.148 = (bf16[2048,896]{1,0:T(8,128)(2,1)}, bf16[512,1024]{1,0:T(8,128)(2,1)}) custom-call(bf16[512,2048]{1,0:T(8,128)(2,1)} %all-gather.3.cloned.1.call-done.x_ref, bf16[512,2048]{1,0:T(8,128)(2,1)} %all-gather.5.cloned.1.call-done.dy_ref, bf16[2048,512]{1,0:T(8,128)(2,1)} %get-tuple-element.14.xt_ref, ...), custom_call_target="tpu_custom_call" | custom-call | flops 3623878656 | bytes 16780288 | tf_op jit(solution)/shard_map/pallas_call | solution.py:167
  146.3 7.4 %shard_map.149 = (bf16[512,2048]{1,0:T(8,128)(2,1)}, bf16[512,2048]{1,0:T(8,128)(2,1)}) custom-call(bf16[512,1024]{1,0:T(8,128)(2,1)} %get-tuple-element.16.act_ref, bf16[2048,896]{1,0:T(8,128)(2,1)} %bitcast.w_ref), custom_call_target="tpu_custom_call" | custom-call | flops 1811939328 | bytes 8912896 | tf_op jit(solution)/shard_map/pallas_call | solution.py:167
  153.7 0.0 reduce-scatter.3.cloned.1.call-update
  153.7 11.8 %all-to-all-start.1 = ((bf16[128,16,896]{2,1,0:T(8,128)(2,1)}), bf16[128,16,896]{2,1,0:T(8,128)(2,1)}, u32[]{:S(2)}, u32[]{:S(2)}) async-start(bf16[128,16,896]{2,1,0:T(8,128)(2,1)} %bitcast.2), calls=%async_computation.3 | async-start | bytes 7340032 | tf_op jit(solution)/shard_map/all_to_all | solution.py:232
  165.5 0.0 reduce-scatter.5.cloned.1.call-start
  165.6 0.5 reduce-scatter.5.cloned.1.call-update
  166.1 86.2 %all-to-all-done.1.recv_ref = bf16[128,16,896]{2,1,0:T(8,128)(2,1)} async-done(((bf16[128,16,896]{2,1,0:T(8,128)(2,1)}), bf16[128,16,896]{2,1,0:T(8,128)(2,1)}, u32[]{:S(2)}, u32[]{:S(2)}) %all-to-all-start.1) | async-done | bytes 3670048 | tf_op jit(solution)/shard_map/all_to_all | solution.py:232
  252.3 18.3 %shard_map.150 = (bf16[16,96,128]{2,1,0:T(8,128)(2,1)}, bf16[16,96,128]{2,1,0:T(8,128)(2,1)}, bf16[16,96,128]{2,1,0:T(8,128)(2,1)}) custom-call(s32[384]{0:T(512)} %reshape.23.hits_ref, bf16[128,16,896]{2,1,0:T(8,128)(2,1)} %all-to-all-done.1.recv_ref), custom_call_target="tpu_custom_call" | custom-call | bytes 4851200 | tf_op jit(solution)/shard_map/pallas_call | solution.py:167
  270.6 0.0 reduce-scatter.3.cloned.1.call-done
  270.6 0.0 reduce-scatter.5.cloned.1.call-done
  (3 shorter events, 0.0 us)
Async XLA Ops:
  28.2 19.7 %copy-start.1 = (s32[128,2]{0,1:T(2,128)S(1)}, s32[128,2]{0,1:T(2,128)}, u32[]{:S(2)}) copy-start(s32[128,2]{0,1:T(2,128)} %param.13) | copy-start | bytes 3076
  28.2 19.8 %copy-start = (s32[128,2]{0,1:T(2,128)S(1)}, s32[128,2]{0,1:T(2,128)}, u32[]{:S(2)}) copy-start(s32[128,2]{0,1:T(2,128)} %param.12) | copy-start | bytes 3076
  28.2 104.8 %all-to-all-start = ((bf16[128,16,896]{2,1,0:T(8,128)(2,1)}), bf16[128,16,896]{2,1,0:T(8,128)(2,1)}, u32[]{:S(2)}, u32[]{:S(2)}) async-start(bf16[128,16,896]{2,1,0:T(8,128)(2,1)} %shard_map.147), calls=%async_computation | async-start | bytes 7340032 | tf_op jit(solution)/shard_map/all_to_all | solution.py:219
  46.4 39.6 %all-gather.3.cloned.1.call-start = ((), (), s32[]{:S(2)}) async-start(), calls=%async_computation.4 | async-start | bytes 2621440 | tf_op jit(solution)/shard_map/all_gather | solution.py:220
  47.1 77.2 %all-gather.5.cloned.1.call-start = ((), (), s32[]{:S(2)}) async-start(), calls=%async_computation.5 | async-start | bytes 2621440 | tf_op jit(solution)/shard_map/all_gather | solution.py:221
  47.9 222.7 %reduce-scatter.3.cloned.1.call-start = ((), (), s32[]{:S(2)}) async-start(), calls=%async_computation.6 | async-start | bytes 2621440 | tf_op jit(solution)/shard_map/reduce_scatter | solution.py:238
  153.7 98.6 %all-to-all-start.1 = ((bf16[128,16,896]{2,1,0:T(8,128)(2,1)}), bf16[128,16,896]{2,1,0:T(8,128)(2,1)}, u32[]{:S(2)}, u32[]{:S(2)}) async-start(bf16[128,16,896]{2,1,0:T(8,128)(2,1)} %bitcast.2), calls=%async_computation.3 | async-start | bytes 7340032 | tf_op jit(solution)/shard_map/all_to_all | solution.py:232
  165.5 105.0 %reduce-scatter.5.cloned.1.call-start = ((), (), s32[]{:S(2)}) async-start(), calls=%async_computation.7 | async-start | bytes 2621440 | tf_op jit(solution)/shard_map/reduce_scatter | solution.py:239
Sparse Core Ops, SparseCore 0:
  49.3 36.5 all-gather.2
  88.1 36.2 all-gather.4
  153.8 31.8 reduce-scatter.2
  189.3 34.7 reduce-scatter.4
where the time goes:
time: 278 us; the launch traced here: 277 us
  waiting for transfers between devices  156 us (56%)
  Pallas kernels  63.8 us (23%)
  starting transfers between devices  30.2 us (11%)
  between operations  13.8 us (5%)
  blocking collectives  11.1 us (4%)
    all_to_all x1, waiting for transfers between devices, per_device(): lax.all_to_all(terms.reshape(groups, owner_rows, 896), 'wide', split_axis...  86.2 us
    pallas_call x5, Pallas kernels, vmem_call(): pl.pallas_call(body, out_shape=out_shapes, in_specs=[scalar] * smem + [in...  63.8 us
    all_gather x1, waiting for transfers between devices, per_device(): group_dy = lax.all_gather(cotangent, 'narrow', axis=0, tiled=True)  38.4 us
    all_gather x1, waiting for transfers between devices, per_device(): group_x = lax.all_gather(tokens, 'narrow', axis=0, tiled=True)  26.8 us
    all_to_all x1, starting transfers between devices, per_device(): lax.all_to_all(sent, 'wide', split_axis=0, concat_axis=0, tiled=True)  18.2 us
    all_to_all x1, starting transfers between devices, per_device(): lax.all_to_all(terms.reshape(groups, owner_rows, 896), 'wide', split_axis...  11.8 us
    all_gather x1, blocking collectives, per_device(): group_rw = lax.all_gather(rweight, 'narrow', axis=0, tiled=True)  11.1 us
  transfers between devices with their start and end apart: 6, of which 4 were waited for; matrix products, arithmetic and copies ran while one was open for 0% of the time, Pallas kernels for 9%

commit v1 on v0

v1 whole, which is shorter than its diff:
```python
import jax
import jax.numpy as jnp
from jax import lax
from jax.experimental import pallas as pl
from jax.experimental.pallas import tpu as pltpu
from jax.sharding import PartitionSpec as P

LANES = 128
MIB = 1024 * 1024
PARTS = 8

COLUMNS = 896


def lane_index(shape):
    return lax.broadcasted_iota(jnp.int32, shape, len(shape) - 1)


def batched(count, size, load, store):
    @pl.loop(0, count // size)
    def _(i):
        values = [load(i * size + j) for j in range(size)]
        for j in range(size):
            store(i * size + j, values[j])


def pack_kernel(hits_ref, gate_ref, up_ref, down_ref, gs_ref, us_ref, ds_ref, out_ref, held, wide, ready, sem):
    rows, block, experts = gate_ref.shape
    groups = out_ref.shape[0]
    for m, s_ref in enumerate((gs_ref, us_ref, ds_ref)):
        wide[m] = s_ref[...].astype(jnp.float32)

    def scaled(r):
        flipped = []
        for m, w_ref in enumerate((gate_ref, up_ref, down_ref)):
            w = (w_ref[r].astype(jnp.float32) * wide[m, pl.ds(r, 1), :]).astype(jnp.bfloat16)
            w = jnp.concatenate([w, jnp.zeros((LANES - block, experts), jnp.bfloat16)], axis=0)
            flipped.append(w.astype(jnp.float32).T)
        return flipped

    def keep(r, flipped):
        for m in range(3):
            held[m, pl.ds(r, experts, stride=rows), :] = flipped[m]

    batched(rows, 4, scaled, keep)
    lane = lane_index((rows, LANES))

    def message(g):
        tiles, tail = [], jnp.zeros((rows, LANES), jnp.bfloat16)
        starts = [pl.multiple_of(hits_ref[k, g] * rows, rows) for k in range(3)]
        for m in range(3):
            first, second, third = [held[m, pl.ds(s, rows), :].astype(jnp.bfloat16) for s in starts]
            moved = pltpu.roll(second, 96, 1)
            last = pltpu.roll(third, 64, 1)
            tiles.append(jnp.where(lane < 96, first, moved))
            tiles.append(jnp.where(lane < 64, moved, last))
            rest = last if m == 0 else third if m == 2 else pltpu.roll(third, 96, 1)
            tail = jnp.where((lane >= 32 * m) & (lane < 32 * m + 32), rest, tail)
        return tiles + [tail]

    def emit(g, tiles):
        for q, tile in enumerate(tiles):
            ready[g, :, LANES * q : LANES * q + LANES] = tile

    size = groups // PARTS

    def move(i):
        part = pl.ds(i * size, size)
        return pltpu.make_async_copy(ready.at[part], out_ref.at[part], sem.at[i])

    for i in range(PARTS):
        batched(size, 4, lambda g, i=i: message(i * size + g), lambda g, t, i=i: emit(i * size + g, t))
        move(i).start()
    for i in range(PARTS):
        move(i).wait()


def settle_kernel(places_ref, recv_ref, gate_ref, up_ref, down_ref, here, norm, acc, sem):
    rows, block, experts = gate_ref.shape
    groups = recv_ref.shape[0]
    size = groups // PARTS

    def move(i):
        part = pl.ds(i * size, size)
        return pltpu.make_async_copy(recv_ref.at[part], here.at[part], sem.at[i])

    for i in range(PARTS):
        move(i).start()
    lane = lane_index((rows, LANES))

    def terms(g):
        tail = here[g, :, 768:896]
        out = []
        for m in range(3):
            low = here[g, :, 256 * m : 256 * m + 128]
            high = here[g, :, 256 * m + 128 : 256 * m + 256]
            second = pltpu.roll(jnp.where(lane < 64, high, low), 32, 1)
            if m == 0:
                third = pltpu.roll(jnp.where(lane < 64, tail, high), 64, 1)
            else:
                rest = tail if m == 2 else pltpu.roll(tail, 32, 1)
                third = jnp.where(lane < 64, pltpu.roll(high, 64, 1), rest)
            out.append((low, second, third))
        return out

    def keep(g, out):
        for m in range(3):
            for k in range(3):
                norm[m, 3 * g + k] = out[m][k]

    for i in range(PARTS):
        move(i).wait()
        batched(size, 4, lambda g, i=i: terms(i * size + g), lambda g, t, i=i: keep(i * size + g, t))

    def total(e):
        spots = [places_ref[q, e] for q in range(3)]
        out = []
        for m in range(3):
            a, b, c = [norm[m, s].astype(jnp.float32) for s in spots]
            out.append(a + b + c)
        return out

    def put(e, out):
        for m in range(3):
            acc[m, pl.ds(pl.multiple_of(e * rows, rows), rows), :] = out[m]

    batched(experts, 8, total, put)
    refs = (gate_ref, up_ref, down_ref)

    def flipped(r):
        return [acc[m, pl.ds(r, experts, stride=rows), :].T[:block].astype(jnp.bfloat16) for m in range(3)]

    def finish(r, out):
        for m in range(3):
            refs[m][r] = out[m]

    batched(rows, 4, flipped, finish)


def dot(left, right):
    return lax.dot_general(left, right, (((1,), (0,)), ((), ())), preferred_element_type=jnp.float32)


def dot_t(left, right):
    return lax.dot_general(left, right, (((1,), (1,)), ((), ())), preferred_element_type=jnp.float32)


def middle_kernel(x_ref, dy_ref, xt_ref, dyt_ref, rw_ref, w_ref, term_ref, act_ref, here, ready, in_sem, out_sem):
    tok, width = x_ref.shape
    spans = ((0, 256), (256, 256), (768, 128), (512, 256))

    def fetch(i):
        cols = pl.ds(*spans[i])
        return pltpu.make_async_copy(w_ref.at[:, cols], here.at[:, cols], in_sem.at[i])

    for i in range(4):
        fetch(i).start()
    rw = rw_ref[...].astype(jnp.float32)

    def finish(gate, up, back, share):
        sig = jax.nn.sigmoid(gate)
        silu = gate * sig
        weighted = share * silu * up
        d_act = share * back
        d_gate = d_act * up * sig * (1.0 + gate * (1.0 - sig))
        return d_gate, d_act * silu, weighted

    fetch(0).wait()
    gate = dot(x_ref[...], here[:, 0:256])
    fetch(1).wait()
    up = dot(x_ref[...], here[:, 256:512])
    fetch(2).wait()
    tail_x = dot(x_ref[...], here[:, 768:896])
    tail_dy = dot(dy_ref[...], here[:, 768:896])
    fetch(3).wait()
    back = dot(dy_ref[...], here[:, 512:768])
    lane = lane_index((tok, LANES))
    d_gate, d_up, weighted = finish(tail_x, pltpu.roll(tail_x, 96, 1), pltpu.roll(tail_dy, 64, 1), rw[:, 2:3])
    from_x = jnp.where(lane < 32, d_gate, jnp.where(lane < 64, pltpu.roll(d_up, 32, 1), 0.0))
    from_dy = jnp.where((lane >= 64) & (lane < 96), pltpu.roll(weighted, 64, 1), 0.0)
    act_ref[:, 768:896] = from_x.astype(jnp.bfloat16)
    act_ref[:, 896:1024] = from_dy.astype(jnp.bfloat16)
    lane = lane_index((tok, 256))
    share = jnp.where(lane < 96, rw[:, 0:1], jnp.where(lane < 192, rw[:, 1:2], rw[:, 2:3]))
    d_gate, d_up, weighted = finish(gate, up, back, share)
    act_ref[:, 0:256] = d_gate.astype(jnp.bfloat16)
    act_ref[:, 256:512] = d_up.astype(jnp.bfloat16)
    act_ref[:, 512:768] = weighted.astype(jnp.bfloat16)
    size = 512

    def send(i):
        part = pl.ds(pl.multiple_of(i * size, size), size)
        return pltpu.make_async_copy(ready.at[part], term_ref.at[part], out_sem.at[i])

    @pl.loop(0, width // size)
    def _(i):
        cols = pl.ds(pl.multiple_of(i * size, size), size)
        xt = xt_ref[cols, :]
        dyt = dyt_ref[cols, :]
        ready[cols, 0:256] = dot(xt, act_ref[:, 0:256]).astype(jnp.bfloat16)
        ready[cols, 256:512] = dot(xt, act_ref[:, 256:512]).astype(jnp.bfloat16)
        ready[cols, 512:768] = dot(dyt, act_ref[:, 512:768]).astype(jnp.bfloat16)
        tail = dot(xt, act_ref[:, 768:896]) + dot(dyt, act_ref[:, 896:1024])
        ready[cols, 768:896] = tail.astype(jnp.bfloat16)
        send(i).start()

    for i in range(width // size):
        send(i).wait()


def out_kernel(act_ref, w_ref, *outs):
    width = w_ref.shape[0]
    size = outs[0].shape[0]

    @pl.loop(0, width // 512)
    def _(i):
        start = pl.multiple_of(i * 512, 512)
        cols = pl.ds(start, 512)
        tail = w_ref[cols, 768:896]
        mixed = dot_t(act_ref[:, 512:768], w_ref[cols, 512:768]) + dot_t(act_ref[:, 896:1024], tail)
        grad = dot_t(act_ref[:, 0:512], w_ref[cols, 0:512]) + dot_t(act_ref[:, 768:896], tail)
        for s, out_ref in enumerate(outs):
            part = slice(s * size, s * size + size)
            out_ref[:, cols] = mixed[part].astype(jnp.bfloat16)
            out_ref[:, pl.ds(pl.multiple_of(start + width, 512), 512)] = grad[part].astype(jnp.bfloat16)


def flip_kernel(hits_ref, *refs):
    *blocks, places_ref, x_ref, dy_ref, xt_ref, dyt_ref, rw_ref, count = refs
    slots, groups = hits_ref.shape
    experts = places_ref.shape[1]
    size = blocks[0].shape[0]
    width = x_ref.shape[1]
    for s, ref in enumerate(blocks):
        rows = pl.ds(s * size, size)
        x_ref[rows, :] = ref[:, 0:width]
        dy_ref[rows, :] = ref[:, width : 2 * width]
        rw_ref[rows, :] = ref[:, 2 * width :]

    @pl.loop(0, width // 512)
    def _(i):
        cols = pl.ds(pl.multiple_of(i * 512, 512), 512)
        xt_ref[cols, :] = x_ref[:, cols].T
        dyt_ref[cols, :] = dy_ref[:, cols].T

    @pl.loop(0, experts)
    def _(e):
        count[e] = 0

    @pl.loop(0, groups)
    def _(g):
        for k in range(slots):
            e = hits_ref[k, g]
            seen = count[e]
            places_ref[seen, e] = slots * g + k
            count[e] = seen + 1


def call(body, outputs, inputs, spaces, out_spaces, scratch=(), limit=16, flops=0):
    moved = sum(a.size * a.dtype.itemsize for a in (*inputs, *outputs))
    return pl.pallas_call(
        body,
        out_shape=outputs,
        in_specs=[pl.BlockSpec(memory_space=s) for s in spaces],
        out_specs=[pl.BlockSpec(memory_space=s) for s in out_spaces],
        scratch_shapes=list(scratch),
        compiler_params=pltpu.CompilerParams(vmem_limit_bytes=limit * MIB),
        cost_estimate=pl.CostEstimate(flops=flops, bytes_accessed=moved, transcendentals=0),
    )(*inputs)


VMEM, SMEM, ANY = pltpu.VMEM, pltpu.SMEM, pl.ANY


def shape(*dims):
    return jax.ShapeDtypeStruct(dims, jnp.bfloat16)


def pack(hits, weights, scales):
    rows, _, experts = weights[0].shape
    groups = hits.shape[1]
    scratch = (
        VMEM((3, rows * experts, LANES), jnp.float32),
        VMEM((3, rows, experts), jnp.float32),
        VMEM((groups, rows, COLUMNS), jnp.bfloat16),
        pltpu.SemaphoreType.DMA((PARTS,)),
    )
    return call(
        pack_kernel,
        [shape(groups, rows, COLUMNS)],
        (hits, *weights, *scales),
        [SMEM] + [VMEM] * 6,
        [ANY],
        scratch,
        limit=60,
    )[0]


def settle(places, received, like):
    rows, _, experts = like.shape
    groups = received.shape[0]
    scratch = (
        VMEM((groups, rows, COLUMNS), jnp.bfloat16),
        VMEM((3, 3 * groups, rows, LANES), jnp.bfloat16),
        VMEM((3, experts * rows, LANES), jnp.float32),
        pltpu.SemaphoreType.DMA((PARTS,)),
    )
    return call(
        settle_kernel, [shape(*like.shape)] * 3, (places, received), [SMEM, ANY], [VMEM] * 3, scratch, limit=60
    )


def middle(x, dy, xt, dyt, rw, weights):
    tok, width = x.shape
    scratch = (
        VMEM((width, COLUMNS), jnp.bfloat16),
        VMEM((width, COLUMNS), jnp.bfloat16),
        pltpu.SemaphoreType.DMA((4,)),
        pltpu.SemaphoreType.DMA((width // 512,)),
    )
    return call(
        middle_kernel,
        [shape(width, COLUMNS), shape(tok, 1024)],
        (x, dy, xt, dyt, rw, weights),
        [VMEM] * 5 + [ANY],
        [ANY, VMEM],
        scratch,
        limit=32,
        flops=2 * 6 * tok * width * 288,
    )


def outputs(act, weights, devices):
    tok = act.shape[0]
    width = weights.shape[0]
    return call(
        out_kernel,
        [shape(tok // devices, 2 * width)] * devices,
        (act, weights),
        [VMEM] * 2,
        [VMEM] * devices,
        limit=60,
        flops=2 * 3 * tok * width * 288,
    )


def flip(hits, blocks, width, experts):
    tok = blocks[0].shape[0] * len(blocks)
    return call(
        flip_kernel,
        [jax.ShapeDtypeStruct((hits.shape[0], experts), jnp.int32)]
        + [shape(tok, width)] * 2
        + [shape(width, tok)] * 2
        + [shape(tok, LANES)],
        (hits, *blocks),
        [SMEM] + [VMEM] * len(blocks),
        [SMEM] + [VMEM] * 5,
        (SMEM((experts,), jnp.int32),),
        limit=60,
    )


def per_device(
    tokens,
    route_slot,
    route_code,
    group_hits,
    gate_w,
    up_w,
    down_w,
    gate_scale,
    up_scale,
    down_scale,
    cotangent,
):
    hit_count = group_hits.shape[1]
    groups = group_hits.shape[0]
    devices = lax.axis_size("narrow")
    owner_rows, _, experts = gate_w.shape
    width = tokens.shape[1]
    hits = group_hits.T
    codes = route_code.astype(jnp.float32)
    shares = codes / jnp.sum(codes, axis=1, keepdims=True)
    slots = jnp.arange(LANES, dtype=jnp.int32)
    picked = (route_slot[:, :, None] == slots[None, None, :]).astype(jnp.float32)
    rweight = jnp.sum(picked * shares[:, :, None], axis=1).astype(jnp.bfloat16)
    sent = pack(hits, (gate_w, up_w, down_w), (gate_scale, up_scale, down_scale))
    received = lax.all_to_all(sent, "wide", split_axis=0, concat_axis=0, tiled=True)
    weights = received.reshape(width, COLUMNS)

    def shift(value, step):
        return lax.ppermute(value, "narrow", [(i, (i + step) % devices) for i in range(devices)])

    mine = jnp.concatenate([tokens, cotangent, rweight], axis=1)
    blocks = [mine] + [shift(mine, s) for s in range(1, devices)]
    places, *gathered = flip(hits, blocks, width, experts)
    terms, act = middle(*gathered, weights)
    back = lax.all_to_all(
        terms.reshape(groups, owner_rows, COLUMNS), "wide", split_axis=0, concat_axis=0, tiled=True
    )
    parts = outputs(act, weights, devices)
    parts = [parts[0]] + [shift(parts[s], devices - s) for s in range(1, devices)]
    total = sum(p.astype(jnp.float32) for p in parts).astype(jnp.bfloat16)
    mixed, token_grad = total[:, :width], total[:, width:]
    gate_grad, up_grad, down_grad = settle(places, back, gate_w)
    return (mixed, token_grad, gate_grad, up_grad, down_grad)


def solution(mesh):
    placed = (
        P(("wide", "narrow"), None),
        P(("wide", "narrow"), None),
        P(("wide", "narrow"), None),
        P(),
        P("wide", "narrow", None),
        P("wide", "narrow", None),
        P("wide", "narrow", None),
        P("wide", None),
        P("wide", None),
        P("wide", None),
        P(("wide", "narrow"), None),
    )
    return jax.shard_map(
        per_device,
        mesh=mesh,
        in_specs=placed,
        out_specs=(
            P(("wide", "narrow"), None),
            P(("wide", "narrow"), None),
            P("wide", "narrow", None),
            P("wide", "narrow", None),
            P("wide", "narrow", None),
        ),
        check_vma=False,
    )
```

time: 278 us -> 237 us (0.85)
  the two profiles are of different devices: /device:TPU:25 before, /device:TPU:29 now
where the time goes in v1:
time: 237 us; the launch traced here: 236 us
  waiting for transfers between devices  135 us (57%)
  starting transfers between devices  43.5 us (18%)
  Pallas kernels  43.1 us (18%)
  local copies, waits for them, and re-layouts  11.2 us (5%)
    ppermute x6, waiting for transfers between devices, shift(): lax.ppermute(value, 'narrow', [(i, (i + step) % devices) for i in range(d...  91.1 us
    pallas_call x5, Pallas kernels, call(): pl.pallas_call(body, out_shape=outputs, in_specs=[pl.BlockSpec(memory_spa...  43.1 us
    all_to_all x1, waiting for transfers between devices, per_device(): lax.all_to_all(terms.reshape(groups, owner_rows, COLUMNS), 'wide', split_...  22.7 us
    all_to_all x1, waiting for transfers between devices, per_device(): lax.all_to_all(sent, 'wide', split_axis=0, concat_axis=0, tiled=True)  21.5 us
    all_to_all x1, starting transfers between devices, per_device(): lax.all_to_all(sent, 'wide', split_axis=0, concat_axis=0, tiled=True)  18.2 us
    ppermute x6, starting transfers between devices, shift(): lax.ppermute(value, 'narrow', [(i, (i + step) % devices) for i in range(d...  16.9 us
    unnamed x28, local copies, waits for them, and re-layouts  10.2 us
    all_to_all x1, starting transfers between devices, per_device(): lax.all_to_all(terms.reshape(groups, owner_rows, COLUMNS), 'wide', split_...  8.45 us
  transfers between devices with their start and end apart: 8, of which 8 were waited for; matrix products, arithmetic and copies ran while one was open for 1% of the time, Pallas kernels for 8%

profile of v1, /device:TPU:29, one launch (start us, length us, event | category | flops | bytes accessed | tf_op | source)
XLA Modules:
  0.0 236.1 jit_solution(8504351318395783979)
XLA Ops:
  0.6 7.0 %shard_map.147 = bf16[128,16,896]{2,1,0:T(8,128)(2,1)} custom-call(s32[3,128]{1,0:T(4,128)} %bitcast.4, bf16[16,96,128]{2,1,0:T(8,128)(2,1)} %gate_ref.1, bf16[16,96,128]{2,1,0:T(8,128)(2,1)} %up_ref.1, bf16[16,96,128]{2,1,0:T(8,128)(2,1)} %down_ref.1, bf16[16,128]{1,0:T(8,128)(2,1)} %gs_ref.1, bf16[16,128]{1,0:T(8,128)(2,1)} %us_ref.1, bf16[16,128]{1,0:T(8,128)(2,1)} %ds_ref.1), custom_call_target="tpu_custom_call" | custom-call | bytes 4863488 | tf_op jit(solution)/shard_map/pallas_call | solution.py:261
  7.7 0.0 copy-start.13
  7.7 0.0 copy-start.12
  7.7 0.0 copy-start.10
  7.7 0.0 copy-start.11
  7.7 18.2 %all-to-all-start = ((bf16[128,16,896]{2,1,0:T(8,128)(2,1)}), bf16[128,16,896]{2,1,0:T(8,128)(2,1)}, u32[]{:S(2)}, u32[]{:S(2)}) async-start(bf16[128,16,896]{2,1,0:T(8,128)(2,1)} %shard_map.147), calls=%async_computation | async-start | bytes 7340032 | tf_op jit(solution)/shard_map/all_to_all | solution.py:388
  25.9 0.0 copy-done.13
  26.0 0.0 copy-done.12
  26.0 0.1 select_reduce_fusion
  26.1 0.0 copy-done.10
  26.1 0.0 copy-done.11
  26.2 0.1 pad_maximum_fusion.refs_0_
  26.2 0.0 copy-start.7
  26.3 2.2 collective-permute-start.2
  28.4 4.4 %collective-permute-start.1 = (bf16[128,4224]{1,0:T(8,128)(2,1)S(1)}, bf16[128,4224]{1,0:T(8,128)(2,1)S(1)}, u32[]{:S(2)}, u32[]{:S(2)}) collective-permute-start(bf16[128,4224]{1,0:T(8,128)(2,1)S(1)} %pad_maximum_fusion.refs_0_), channel_id=1, source_target_pairs={{0,2},{1,3},{2,0},{3,1},{4,6},{5,7},{6,4},{7,5},{8,10},{9,11},{10,... | collective-permute-start | bytes 3244040 | tf_op jit(solution)/shard_map/ppermute | solution.py:392
  32.8 1.9 collective-permute-start
  34.7 18.6 %collective-permute-done.2.refs_3_ = bf16[128,4224]{1,0:T(8,128)(2,1)S(1)} collective-permute-done((bf16[128,4224]{1,0:T(8,128)(2,1)S(1)}, bf16[128,4224]{1,0:T(8,128)(2,1)S(1)}, u32[]{:S(2)}, u32[]{:S(2)}) %collective-permute-start.2) | collective-permute-done | bytes 1081376 | tf_op jit(solution)/shard_map/ppermute | solution.py:392
  53.3 0.0 copy-start.8
  53.3 3.4 %collective-permute-done.1.refs_2_ = bf16[128,4224]{1,0:T(8,128)(2,1)S(1)} collective-permute-done((bf16[128,4224]{1,0:T(8,128)(2,1)S(1)}, bf16[128,4224]{1,0:T(8,128)(2,1)S(1)}, u32[]{:S(2)}, u32[]{:S(2)}) %collective-permute-start.1) | collective-permute-done | bytes 1081376 | tf_op jit(solution)/shard_map/ppermute | solution.py:392
  56.7 0.0 copy-start.9
  56.7 24.1 %collective-permute-done.refs_1_ = bf16[128,4224]{1,0:T(8,128)(2,1)} collective-permute-done((bf16[128,4224]{1,0:T(8,128)(2,1)S(1)}, bf16[128,4224]{1,0:T(8,128)(2,1)}, u32[]{:S(2)}, u32[]{:S(2)}) %collective-permute-start) | collective-permute-done | bytes 1081376 | tf_op jit(solution)/shard_map/ppermute | solution.py:392
  80.9 0.0 copy-done.7
  80.9 0.0 copy-done.8
  80.9 0.0 copy-done.9
  80.9 10.2 %shard_map.146 = (s32[3,128]{1,0:T(4,128)}, bf16[512,2048]{1,0:T(8,128)(2,1)}, bf16[512,2048]{1,0:T(8,128)(2,1)}, bf16[2048,512]{1,0:T(8,128)(2,1)}, bf16[2048,5...) custom-call(s32[3,128]{1,0:T(4,128)} %bitcast.5, bf16[128,4224]{1,0:T(8,128)(2,1)} %copy-done.7, ...), custom_call_target="tpu_custom_call" | custom-call | bytes 12848128 | tf_op jit(solution)/shard_map/pallas_call | solution.py:261
  91.1 21.5 %all-to-all-done = bf16[128,16,896]{2,1,0:T(8,128)(2,1)} async-done(((bf16[128,16,896]{2,1,0:T(8,128)(2,1)}), bf16[128,16,896]{2,1,0:T(8,128)(2,1)}, u32[]{:S(2)}, u32[]{:S(2)}) %all-to-all-start) | async-done | bytes 3670048 | tf_op jit(solution)/shard_map/all_to_all | solution.py:388
  112.6 0.0 copy-start.1
  112.6 1.6 copy-done.1
  114.2 1.6 copy-done.2
  115.8 1.6 copy-done.3
  117.4 1.6 copy-done.4
  118.9 0.9 copy-done.5
  119.9 10.2 %shard_map.148 = (bf16[2048,896]{1,0:T(8,128)(2,1)S(1)}, bf16[512,1024]{1,0:T(8,128)(2,1)S(1)}) custom-call(bf16[512,2048]{1,0:T(8,128)(2,1)S(1)} %copy-done.1, bf16[512,2048]{1,0:T(8,128)(2,1)S(1)} %copy-done.2, bf16[2048,512]{1,0:T(8,128)(2,1)S(1)} %copy-done.3, bf16[2048,512]{1,0:T(8,128)(2,1)S(1)} %copy-done.4, bf16[512,128]{1,0:T(8,128)(2,1)S(1)} %copy-done.5, ...), custom_call_target="tpu_custom_call" | custom-call | flops 3623878656 | bytes 16908288 | tf_op jit(solution)/shard_map/pallas_call | solution.py:261
  130.0 0.0 copy-start
  130.1 1.9 copy-done
  132.0 1.0 copy-done.6
  132.9 8.4 %all-to-all-start.1 = ((bf16[128,16,896]{2,1,0:T(8,128)(2,1)}), bf16[128,16,896]{2,1,0:T(8,128)(2,1)}, u32[]{:S(2)}, u32[]{:S(2)}) async-start(bf16[128,16,896]{2,1,0:T(8,128)(2,1)} %bitcast.3), calls=%async_computation.1 | async-start | bytes 7340032 | tf_op jit(solution)/shard_map/all_to_all | solution.py:398
  141.4 7.6 %shard_map.149 = (bf16[128,4096]{1,0:T(8,128)(2,1)}, bf16[128,4096]{1,0:T(8,128)(2,1)}, bf16[128,4096]{1,0:T(8,128)(2,1)}, bf16[128,4096]{1,0:T(8,128)(2,1)}) custom-call(bf16[512,1024]{1,0:T(8,128)(2,1)} %copy-done.6, bf16[2048,896]{1,0:T(8,128)(2,1)} %bitcast.1.w_ref), custom_call_target="tpu_custom_call" | custom-call | flops 1811939328 | bytes 8912896 | tf_op jit(solution)/shard_map/pallas_call | solution.py:261
  149.0 2.2 collective-permute-start.3
  151.2 4.4 %collective-permute-start.4 = (bf16[128,4096]{1,0:T(8,128)(2,1)}, bf16[128,4096]{1,0:T(8,128)(2,1)S(1)}, u32[]{:S(2)}, u32[]{:S(2)}) collective-permute-start(bf16[128,4096]{1,0:T(8,128)(2,1)} %get-tuple-element.28), channel_id=1, source_target_pairs={{0,2},{1,3},{2,0},{3,1},{4,6},{5,7},{6,4},{7,5},{8,10},{9,11},{10,... | collective-permute-start | bytes 3145736 | tf_op jit(solution)/shard_map/ppermute | solution.py:392
  155.5 1.9 collective-permute-start.5
  157.4 18.1 %collective-permute-done.3 = bf16[128,4096]{1,0:T(8,128)(2,1)S(1)} collective-permute-done((bf16[128,4096]{1,0:T(8,128)(2,1)}, bf16[128,4096]{1,0:T(8,128)(2,1)S(1)}, u32[]{:S(2)}, u32[]{:S(2)}) %collective-permute-start.3) | collective-permute-done | bytes 1048608 | tf_op jit(solution)/shard_map/ppermute | solution.py:392
  175.6 3.4 %collective-permute-done.4 = bf16[128,4096]{1,0:T(8,128)(2,1)S(1)} collective-permute-done((bf16[128,4096]{1,0:T(8,128)(2,1)}, bf16[128,4096]{1,0:T(8,128)(2,1)S(1)}, u32[]{:S(2)}, u32[]{:S(2)}) %collective-permute-start.4) | collective-permute-done | bytes 1048608 | tf_op jit(solution)/shard_map/ppermute | solution.py:392
  179.0 23.4 %collective-permute-done.5 = bf16[128,4096]{1,0:T(8,128)(2,1)S(1)} collective-permute-done((bf16[128,4096]{1,0:T(8,128)(2,1)}, bf16[128,4096]{1,0:T(8,128)(2,1)S(1)}, u32[]{:S(2)}, u32[]{:S(2)}) %collective-permute-start.5) | collective-permute-done | bytes 1048608 | tf_op jit(solution)/shard_map/ppermute | solution.py:392
  202.4 1.9 add_convert_fusion
  204.3 1.0 fusion
  205.3 22.7 %all-to-all-done.1.recv_ref = bf16[128,16,896]{2,1,0:T(8,128)(2,1)} async-done(((bf16[128,16,896]{2,1,0:T(8,128)(2,1)}), bf16[128,16,896]{2,1,0:T(8,128)(2,1)}, u32[]{:S(2)}, u32[]{:S(2)}) %all-to-all-start.1) | async-done | bytes 3670048 | tf_op jit(solution)/shard_map/all_to_all | solution.py:398
  228.0 8.0 %shard_map.150 = (bf16[16,96,128]{2,1,0:T(8,128)(2,1)}, bf16[16,96,128]{2,1,0:T(8,128)(2,1)}, bf16[16,96,128]{2,1,0:T(8,128)(2,1)}) custom-call(s32[3,128]{1,0:T(4,128)} %get-tuple-element.30.places_ref, bf16[128,16,896]{2,1,0:T(8,128)(2,1)} %all-to-all-done.1.recv_ref), custom_call_target="tpu_custom_call" | custom-call | bytes 4851200 | tf_op jit(solution)/shard_map/pallas_call | solution.py:261
  (7 shorter events, 0.0 us)
Async XLA Ops:
  7.7 18.3 %copy-start.13 = (s32[128,2]{0,1:T(2,128)S(1)}, s32[128,2]{0,1:T(2,128)}, u32[]{:S(2)}) copy-start(s32[128,2]{0,1:T(2,128)} %param.13) | copy-start | bytes 3076
  7.7 18.3 %copy-start.12 = (s32[128,2]{0,1:T(2,128)S(1)}, s32[128,2]{0,1:T(2,128)}, u32[]{:S(2)}) copy-start(s32[128,2]{0,1:T(2,128)} %param.12) | copy-start | bytes 3076
  7.7 18.4 %copy-start.10 = (bf16[128,2048]{1,0:T(8,128)(2,1)S(1)}, bf16[128,2048]{1,0:T(8,128)(2,1)}, u32[]{:S(2)}) copy-start(bf16[128,2048]{1,0:T(8,128)(2,1)} %param.21) | copy-start | bytes 1572868
  7.7 18.4 %copy-start.11 = (bf16[128,2048]{1,0:T(8,128)(2,1)S(1)}, bf16[128,2048]{1,0:T(8,128)(2,1)}, u32[]{:S(2)}) copy-start(bf16[128,2048]{1,0:T(8,128)(2,1)} %param.11) | copy-start | bytes 1572868
  7.7 104.8 %all-to-all-start = ((bf16[128,16,896]{2,1,0:T(8,128)(2,1)}), bf16[128,16,896]{2,1,0:T(8,128)(2,1)}, u32[]{:S(2)}, u32[]{:S(2)}) async-start(bf16[128,16,896]{2,1,0:T(8,128)(2,1)} %shard_map.147), calls=%async_computation | async-start | bytes 7340032 | tf_op jit(solution)/shard_map/all_to_all | solution.py:388
  26.2 54.6 %copy-start.7 = (bf16[128,4224]{1,0:T(8,128)(2,1)}, bf16[128,4224]{1,0:T(8,128)(2,1)S(1)}, u32[]{:S(2)}) copy-start(bf16[128,4224]{1,0:T(8,128)(2,1)S(1)} %pad_maximum_fusion.refs_0_) | copy-start | bytes 3244036
  26.3 27.1 %collective-permute-start.2 = (bf16[128,4224]{1,0:T(8,128)(2,1)S(1)}, bf16[128,4224]{1,0:T(8,128)(2,1)S(1)}, u32[]{:S(2)}, u32[]{:S(2)}) collective-permute-start(bf16[128,4224]{1,0:T(8,128)(2,1)S(1)} %pad_maximum_fusion.refs_0_), channel_id=1, source_target_pairs={{0,3},{1,0},{2,1},{3,2},{4,7},{5,4},{6,5},{7,6},{8,11},{9,8},{10,9... | collective-permute-start | bytes 3244040 | tf_op jit(solution)/shard_map/ppermute | solution.py:392
  28.4 28.3 %collective-permute-start.1 = (bf16[128,4224]{1,0:T(8,128)(2,1)S(1)}, bf16[128,4224]{1,0:T(8,128)(2,1)S(1)}, u32[]{:S(2)}, u32[]{:S(2)}) collective-permute-start(bf16[128,4224]{1,0:T(8,128)(2,1)S(1)} %pad_maximum_fusion.refs_0_), channel_id=1, source_target_pairs={{0,2},{1,3},{2,0},{3,1},{4,6},{5,7},{6,4},{7,5},{8,10},{9,11},{10,... | collective-permute-start | bytes 3244040 | tf_op jit(solution)/shard_map/ppermute | solution.py:392
  32.8 48.1 %collective-permute-start = (bf16[128,4224]{1,0:T(8,128)(2,1)S(1)}, bf16[128,4224]{1,0:T(8,128)(2,1)}, u32[]{:S(2)}, u32[]{:S(2)}) collective-permute-start(bf16[128,4224]{1,0:T(8,128)(2,1)S(1)} %pad_maximum_fusion.refs_0_), channel_id=1, source_target_pairs={{0,1},{1,2},{2,3},{3,0},{4,5},{5,6},{6,7},{7,4},{8,9},{9,10},{10,1... | collective-permute-start | bytes 3244040 | tf_op jit(solution)/shard_map/ppermute | solution.py:392
  53.3 27.5 %copy-start.8 = (bf16[128,4224]{1,0:T(8,128)(2,1)}, bf16[128,4224]{1,0:T(8,128)(2,1)S(1)}, u32[]{:S(2)}) copy-start(bf16[128,4224]{1,0:T(8,128)(2,1)S(1)} %collective-permute-done.2.refs_3_) | copy-start | bytes 3244036
  56.7 24.2 %copy-start.9 = (bf16[128,4224]{1,0:T(8,128)(2,1)}, bf16[128,4224]{1,0:T(8,128)(2,1)S(1)}, u32[]{:S(2)}) copy-start(bf16[128,4224]{1,0:T(8,128)(2,1)S(1)} %collective-permute-done.1.refs_2_) | copy-start | bytes 3244036
  112.6 1.6 copy-start.1
  114.2 1.6 copy-start.2
  115.8 1.6 copy-start.3
  117.4 1.6 copy-start.4
  118.9 0.9 copy-start.5
  130.0 1.9 copy-start
  132.0 1.0 copy-start.6
  132.9 95.1 %all-to-all-start.1 = ((bf16[128,16,896]{2,1,0:T(8,128)(2,1)}), bf16[128,16,896]{2,1,0:T(8,128)(2,1)}, u32[]{:S(2)}, u32[]{:S(2)}) async-start(bf16[128,16,896]{2,1,0:T(8,128)(2,1)} %bitcast.3), calls=%async_computation.1 | async-start | bytes 7340032 | tf_op jit(solution)/shard_map/all_to_all | solution.py:398
  149.0 26.6 %collective-permute-start.3 = (bf16[128,4096]{1,0:T(8,128)(2,1)}, bf16[128,4096]{1,0:T(8,128)(2,1)S(1)}, u32[]{:S(2)}, u32[]{:S(2)}) collective-permute-start(bf16[128,4096]{1,0:T(8,128)(2,1)} %get-tuple-element.27), channel_id=1, source_target_pairs={{0,3},{1,0},{2,1},{3,2},{4,7},{5,4},{6,5},{7,6},{8,11},{9,8},{10,9... | collective-permute-start | bytes 3145736 | tf_op jit(solution)/shard_map/ppermute | solution.py:392
  151.2 27.8 %collective-permute-start.4 = (bf16[128,4096]{1,0:T(8,128)(2,1)}, bf16[128,4096]{1,0:T(8,128)(2,1)S(1)}, u32[]{:S(2)}, u32[]{:S(2)}) collective-permute-start(bf16[128,4096]{1,0:T(8,128)(2,1)} %get-tuple-element.28), channel_id=1, source_target_pairs={{0,2},{1,3},{2,0},{3,1},{4,6},{5,7},{6,4},{7,5},{8,10},{9,11},{10,... | collective-permute-start | bytes 3145736 | tf_op jit(solution)/shard_map/ppermute | solution.py:392
  155.5 46.9 %collective-permute-start.5 = (bf16[128,4096]{1,0:T(8,128)(2,1)}, bf16[128,4096]{1,0:T(8,128)(2,1)S(1)}, u32[]{:S(2)}, u32[]{:S(2)}) collective-permute-start(bf16[128,4096]{1,0:T(8,128)(2,1)} %get-tuple-element.29), channel_id=1, source_target_pairs={{0,1},{1,2},{2,3},{3,0},{4,5},{5,6},{6,7},{7,4},{8,9},{9,10},{10,1... | collective-permute-start | bytes 3145736 | tf_op jit(solution)/shard_map/ppermute | solution.py:392

commit v2 on v1

--- a/solution.py
+++ b/solution.py
@@ -8,6 +8,10 @@
 LANES = 128
 MIB = 1024 * 1024
 PARTS = 8
+STEPS = 4
+AHEAD = 4
+SIZE = 512
+CHUNK = 256
 
 COLUMNS = 896
 
@@ -24,25 +28,31 @@
             store(i * size + j, values[j])
 
 
-def pack_kernel(hits_ref, gate_ref, up_ref, down_ref, gs_ref, us_ref, ds_ref, out_ref, held, wide, ready, sem):
-    rows, block, experts = gate_ref.shape
+def pack_kernel(
+    hits_ref, gate_hbm, up_hbm, down_hbm, gs_ref, us_ref, ds_ref, out_ref, stored, held, wide, ready, in_sem, sem
+):
+    _, rows, block, experts = stored.shape
     groups = out_ref.shape[0]
+    fetches = [
+        pltpu.make_async_copy(w_hbm, stored.at[m], in_sem.at[m])
+        for m, w_hbm in enumerate((gate_hbm, up_hbm, down_hbm))
+    ]
+    for copy in fetches:
+        copy.start()
     for m, s_ref in enumerate((gs_ref, us_ref, ds_ref)):
         wide[m] = s_ref[...].astype(jnp.float32)
-
-    def scaled(r):
-        flipped = []
-        for m, w_ref in enumerate((gate_ref, up_ref, down_ref)):
-            w = (w_ref[r].astype(jnp.float32) * wide[m, pl.ds(r, 1), :]).astype(jnp.bfloat16)
+    for m in range(3):
+        fetches[m].wait()
+
+        def scaled(r, m=m):
+            w = (stored[m, r].astype(jnp.float32) * wide[m, pl.ds(r, 1), :]).astype(jnp.bfloat16)
             w = jnp.concatenate([w, jnp.zeros((LANES - block, experts), jnp.bfloat16)], axis=0)
-            flipped.append(w.astype(jnp.float32).T)
-        return flipped
-
-    def keep(r, flipped):
-        for m in range(3):
-            held[m, pl.ds(r, experts, stride=rows), :] = flipped[m]
-
-    batched(rows, 4, scaled, keep)
+            return w.T.astype(jnp.float32)
+
+        def keep(r, flipped, m=m):
+            held[m, pl.ds(r, experts, stride=rows), :] = flipped
+
+        batched(rows, 16, scaled, keep)
     lane = lane_index((rows, LANES))
 
     def message(g):
@@ -69,7 +79,7 @@
         return pltpu.make_async_copy(ready.at[part], out_ref.at[part], sem.at[i])
 
     for i in range(PARTS):
-        batched(size, 4, lambda g, i=i: message(i * size + g), lambda g, t, i=i: emit(i * size + g, t))
+        batched(size, 16, lambda g, i=i: message(i * size + g), lambda g, t, i=i: emit(i * size + g, t))
         move(i).start()
     for i in range(PARTS):
         move(i).wait()
@@ -110,7 +120,7 @@
 
     for i in range(PARTS):
         move(i).wait()
-        batched(size, 4, lambda g, i=i: terms(i * size + g), lambda g, t, i=i: keep(i * size + g, t))
+        batched(size, 16, lambda g, i=i: terms(i * size + g), lambda g, t, i=i: keep(i * size + g, t))
 
     def total(e):
         spots = [places_ref[q, e] for q in range(3)]
@@ -124,17 +134,17 @@
         for m in range(3):
             acc[m, pl.ds(pl.multiple_of(e * rows, rows), rows), :] = out[m]
 
-    batched(experts, 8, total, put)
+    batched(experts, 16, total, put)
     refs = (gate_ref, up_ref, down_ref)
 
     def flipped(r):
-        return [acc[m, pl.ds(r, experts, stride=rows), :].T[:block].astype(jnp.bfloat16) for m in range(3)]
+        return [acc[m, pl.ds(r, experts, stride=rows), :].astype(jnp.bfloat16).T[:block] for m in range(3)]
 
     def finish(r, out):
         for m in range(3):
             refs[m][r] = out[m]
 
-    batched(rows, 4, flipped, finish)
+    batched(rows, 8, flipped, finish)
 
 
 def dot(left, right):
@@ -145,17 +155,47 @@
     return lax.dot_general(left, right, (((1,), (1,)), ((), ())), preferred_element_type=jnp.float32)
 
 
-def middle_kernel(x_ref, dy_ref, xt_ref, dyt_ref, rw_ref, w_ref, term_ref, act_ref, here, ready, in_sem, out_sem):
-    tok, width = x_ref.shape
-    spans = ((0, 256), (256, 256), (768, 128), (512, 256))
-
-    def fetch(i):
-        cols = pl.ds(*spans[i])
-        return pltpu.make_async_copy(w_ref.at[:, cols], here.at[:, cols], in_sem.at[i])
-
-    for i in range(4):
-        fetch(i).start()
-    rw = rw_ref[...].astype(jnp.float32)
+def middle_kernel(
+    x_hbm, dy_hbm, xt_hbm, dyt_hbm, rw_hbm, w_hbm, term_ref, act_ref, x, dy, xt, dyt, rw, w, act, ready, pre, sem, flip_sem, out_sem
+):
+    tok, width = x.shape
+
+    steps = STEPS
+    depth = width // steps
+
+    def arriving(i):
+        part = pl.ds(i * depth, depth)
+        pairs = ((x_hbm.at[:, part], x.at[:, part]), (dy_hbm.at[:, part], dy.at[:, part]), (w_hbm.at[part], w.at[part]))
+        return [pltpu.make_async_copy(*pair, sem.at[3 * i + j]) for j, pair in enumerate(pairs)]
+
+    def flipped(i):
+        part = pl.ds(i * size, size)
+        pairs = ((xt_hbm.at[part], xt.at[part]), (dyt_hbm.at[part], dyt.at[part]))
+        return [pltpu.make_async_copy(*pair, flip_sem.at[2 * i + j]) for j, pair in enumerate(pairs)]
+
+    size = SIZE
+    waiting = [arriving(i) for i in range(steps)]
+    waiting.append([pltpu.make_async_copy(rw_hbm, rw, sem.at[3 * steps])])
+    waiting += [flipped(i) for i in range(width // size)]
+    for group in waiting[:AHEAD]:
+        for copy in group:
+            copy.start()
+    started = AHEAD
+    for i in range(steps):
+        for copy in waiting[i]:
+            copy.wait()
+        for copy in waiting[started] if started < len(waiting) else ():
+            copy.start()
+        started += 1
+        part = pl.ds(i * depth, depth)
+        for left, cols in ((x, slice(0, 512)), (x, slice(768, 896)), (dy, slice(512, 768)), (dy, slice(768, 896))):
+            to = slice(896, 1024) if left is dy and cols.start == 768 else cols
+            term = dot(left[:, part], w[part, cols])
+            pre[:, to] = term if i == 0 else pre[:, to] + term
+    for group in waiting[started:]:
+        for copy in group:
+            copy.start()
+    waiting[steps][0].wait()
 
     def finish(gate, up, back, share):
         sig = jax.nn.sigmoid(gate)
@@ -165,45 +205,45 @@
         d_gate = d_act * up * sig * (1.0 + gate * (1.0 - sig))
         return d_gate, d_act * silu, weighted
 
-    fetch(0).wait()
-    gate = dot(x_ref[...], here[:, 0:256])
-    fetch(1).wait()
-    up = dot(x_ref[...], here[:, 256:512])
-    fetch(2).wait()
-    tail_x = dot(x_ref[...], here[:, 768:896])
-    tail_dy = dot(dy_ref[...], here[:, 768:896])
-    fetch(3).wait()
-    back = dot(dy_ref[...], here[:, 512:768])
-    lane = lane_index((tok, LANES))
-    d_gate, d_up, weighted = finish(tail_x, pltpu.roll(tail_x, 96, 1), pltpu.roll(tail_dy, 64, 1), rw[:, 2:3])
-    from_x = jnp.where(lane < 32, d_gate, jnp.where(lane < 64, pltpu.roll(d_up, 32, 1), 0.0))
-    from_dy = jnp.where((lane >= 64) & (lane < 96), pltpu.roll(weighted, 64, 1), 0.0)
-    act_ref[:, 768:896] = from_x.astype(jnp.bfloat16)
-    act_ref[:, 896:1024] = from_dy.astype(jnp.bfloat16)
-    lane = lane_index((tok, 256))
-    share = jnp.where(lane < 96, rw[:, 0:1], jnp.where(lane < 192, rw[:, 1:2], rw[:, 2:3]))
-    d_gate, d_up, weighted = finish(gate, up, back, share)
-    act_ref[:, 0:256] = d_gate.astype(jnp.bfloat16)
-    act_ref[:, 256:512] = d_up.astype(jnp.bfloat16)
-    act_ref[:, 512:768] = weighted.astype(jnp.bfloat16)
-    size = 512
+    chunk = CHUNK
+    lane = lane_index((chunk, LANES))
+
+    @pl.loop(0, tok // chunk)
+    def _(i):
+        rows = pl.ds(pl.multiple_of(i * chunk, chunk), chunk)
+        share = rw[rows, :].astype(jnp.float32)
+        one, two, three = share[:, 0:1], share[:, 1:2], share[:, 2:3]
+        for h, part in enumerate((jnp.where(lane < 96, one, two), jnp.where(lane < 64, two, three))):
+            at = [slice(256 * m + 128 * h, 256 * m + 128 * h + 128) for m in range(3)]
+            for span, value in zip(at, finish(*[pre[rows, span] for span in at], part)):
+                act[rows, span] = value.astype(jnp.bfloat16)
+        tail_x, tail_dy = pre[rows, 768:896], pre[rows, 896:1024]
+        d_gate, d_up, weighted = finish(tail_x, pltpu.roll(tail_x, 96, 1), pltpu.roll(tail_dy, 64, 1), three)
+        from_x = jnp.where(lane < 32, d_gate, jnp.where(lane < 64, pltpu.roll(d_up, 32, 1), 0.0))
+        from_dy = jnp.where((lane >= 64) & (lane < 96), pltpu.roll(weighted, 64, 1), 0.0)
+        act[rows, 768:896] = from_x.astype(jnp.bfloat16)
+        act[rows, 896:1024] = from_dy.astype(jnp.bfloat16)
+
+    put_act = pltpu.make_async_copy(act, act_ref, sem.at[3 * steps + 1])
+    put_act.start()
 
     def send(i):
         part = pl.ds(pl.multiple_of(i * size, size), size)
         return pltpu.make_async_copy(ready.at[part], term_ref.at[part], out_sem.at[i])
 
-    @pl.loop(0, width // size)
-    def _(i):
-        cols = pl.ds(pl.multiple_of(i * size, size), size)
-        xt = xt_ref[cols, :]
-        dyt = dyt_ref[cols, :]
-        ready[cols, 0:256] = dot(xt, act_ref[:, 0:256]).astype(jnp.bfloat16)
-        ready[cols, 256:512] = dot(xt, act_ref[:, 256:512]).astype(jnp.bfloat16)
-        ready[cols, 512:768] = dot(dyt, act_ref[:, 512:768]).astype(jnp.bfloat16)
-        tail = dot(xt, act_ref[:, 768:896]) + dot(dyt, act_ref[:, 896:1024])
+    for group in waiting[steps + 1 :]:
+        for copy in group:
+            copy.wait()
+    for i in range(width // size):
+        cols = pl.ds(i * size, size)
+        left, right = xt[cols, :], dyt[cols, :]
+        ready[cols, 0:512] = dot(left, act[:, 0:512]).astype(jnp.bfloat16)
+        ready[cols, 512:768] = dot(right, act[:, 512:768]).astype(jnp.bfloat16)
+        tail = dot(left, act[:, 768:896]) + dot(right, act[:, 896:1024])
         ready[cols, 768:896] = tail.astype(jnp.bfloat16)
         send(i).start()
 
+    put_act.wait()
     for i in range(width // size):
         send(i).wait()
 
@@ -280,16 +320,18 @@
     rows, _, experts = weights[0].shape
     groups = hits.shape[1]
     scratch = (
+        VMEM((3, *weights[0].shape), jnp.bfloat16),
         VMEM((3, rows * experts, LANES), jnp.float32),
         VMEM((3, rows, experts), jnp.float32),
         VMEM((groups, rows, COLUMNS), jnp.bfloat16),
+        pltpu.SemaphoreType.DMA((3,)),
         pltpu.SemaphoreType.DMA((PARTS,)),
     )
     return call(
         pack_kernel,
         [shape(groups, rows, COLUMNS)],
         (hits, *weights, *scales),
-        [SMEM] + [VMEM] * 6,
+        [SMEM] + [ANY] * 3 + [VMEM] * 3,
         [ANY],
         scratch,
         limit=60,
@@ -313,19 +355,22 @@
 def middle(x, dy, xt, dyt, rw, weights):
     tok, width = x.shape
     scratch = (
+        *[VMEM(a.shape, jnp.bfloat16) for a in (x, dy, xt, dyt, rw, weights)],
+        VMEM((tok, 1024), jnp.bfloat16),
         VMEM((width, COLUMNS), jnp.bfloat16),
-        VMEM((width, COLUMNS), jnp.bfloat16),
-        pltpu.SemaphoreType.DMA((4,)),
-        pltpu.SemaphoreType.DMA((width // 512,)),
+        VMEM((tok, 1024), jnp.float32),
+        pltpu.SemaphoreType.DMA((3 * STEPS + 2,)),
+        pltpu.SemaphoreType.DMA((2 * width // SIZE,)),
+        pltpu.SemaphoreType.DMA((width // SIZE,)),
     )
     return call(
         middle_kernel,
         [shape(width, COLUMNS), shape(tok, 1024)],
         (x, dy, xt, dyt, rw, weights),
-        [VMEM] * 5 + [ANY],
-        [ANY, VMEM],
+        [ANY] * 6,
+        [ANY, ANY],
         scratch,
-        limit=32,
+        limit=60,
         flops=2 * 6 * tok * width * 288,
     )
 

time: 237 us -> 223 us (0.941)
  local copies, waits for them, and re-layouts: 11.2 us -> 1.07 us
  Pallas kernels: 43.1 us -> 39.9 us
    unnamed x28 -> x14, local copies, waits for them, and re-layouts: 10.2 us -> 0.04 us
    pallas_call x5, Pallas kernels: 43.1 us -> 39.9 us  [call(): pl.pallas_call(body, out_shape=outputs, in_specs=[pl.BlockSpec(memory_spa...]
where the time goes in v2:
time: 223 us
  waiting for transfers between devices  135 us (61%)
  starting transfers between devices  43.5 us (20%)
  Pallas kernels  39.9 us (18%)
    ppermute x6, waiting for transfers between devices, shift(): lax.ppermute(value, 'narrow', [(i, (i + step) % devices) for i in range(d...  91.1 us
    pallas_call x5, Pallas kernels, call(): pl.pallas_call(body, out_shape=outputs, in_specs=[pl.BlockSpec(memory_spa...  39.9 us
    all_to_all x1, waiting for transfers between devices, per_device(): lax.all_to_all(terms.reshape(groups, owner_rows, COLUMNS), 'wide', split_...  22.5 us
    all_to_all x1, waiting for transfers between devices, per_device(): lax.all_to_all(sent, 'wide', split_axis=0, concat_axis=0, tiled=True)  21.5 us
    all_to_all x1, starting transfers between devices, per_device(): lax.all_to_all(sent, 'wide', split_axis=0, concat_axis=0, tiled=True)  18.2 us
    ppermute x6, starting transfers between devices, shift(): lax.ppermute(value, 'narrow', [(i, (i + step) % devices) for i in range(d...  16.9 us
    all_to_all x1, starting transfers between devices, per_device(): lax.all_to_all(terms.reshape(groups, owner_rows, COLUMNS), 'wide', split_...  8.46 us
  transfers between devices with their start and end apart: 8, of which 8 were waited for; matrix products, arithmetic and copies ran while one was open for 1% of the time, Pallas kernels for 8%

profile of v2, /device:TPU:29, one launch (start us, length us, event | category | flops | bytes accessed | tf_op | source)
XLA Modules:
  0.0 222.7 jit_solution(16158369370925757399)
XLA Ops:
  0.6 5.2 %shard_map.147 = bf16[128,16,896]{2,1,0:T(8,128)(2,1)} custom-call(s32[3,128]{1,0:T(4,128)} %bitcast.4, bf16[16,96,128]{2,1,0:T(8,128)(2,1)} %gate_hbm.1, bf16[16,96,128]{2,1,0:T(8,128)(2,1)} %up_hbm.1, bf16[16,96,128]{2,1,0:T(8,128)(2,1)} %down_hbm.1, bf16[16,128]{1,0:T(8,128)(2,1)} %gs_ref.1, bf16[16,128]{1,0:T(8,128)(2,1)} %us_ref.1, bf16[16,128]{1,0:T(8,128)(2,1)} %ds_ref.1), custom_call_target="tpu_custom_call" | custom-call | bytes 4863488 | tf_op jit(solution)/shard_map/pallas_call | solution.py:301
  5.9 0.0 copy-start.6
  5.9 0.0 copy-start.5
  5.9 0.0 copy-start.3
  5.9 0.0 copy-start.4
  5.9 18.2 %all-to-all-start = ((bf16[128,16,896]{2,1,0:T(8,128)(2,1)}), bf16[128,16,896]{2,1,0:T(8,128)(2,1)}, u32[]{:S(2)}, u32[]{:S(2)}) async-start(bf16[128,16,896]{2,1,0:T(8,128)(2,1)} %shard_map.147), calls=%async_computation | async-start | bytes 7340032 | tf_op jit(solution)/shard_map/all_to_all | solution.py:433
  24.1 0.0 copy-done.6
  24.2 0.0 copy-done.5
  24.2 0.1 select_reduce_fusion
  24.3 0.0 copy-done.3
  24.3 0.0 copy-done.4
  24.3 0.1 pad_maximum_fusion.refs_0_
  24.4 0.0 copy-start
  24.4 2.2 collective-permute-start.2
  26.6 4.4 %collective-permute-start.1 = (bf16[128,4224]{1,0:T(8,128)(2,1)S(1)}, bf16[128,4224]{1,0:T(8,128)(2,1)S(1)}, u32[]{:S(2)}, u32[]{:S(2)}) collective-permute-start(bf16[128,4224]{1,0:T(8,128)(2,1)S(1)} %pad_maximum_fusion.refs_0_), channel_id=1, source_target_pairs={{0,2},{1,3},{2,0},{3,1},{4,6},{5,7},{6,4},{7,5},{8,10},{9,11},{10,... | collective-permute-start | bytes 3244040 | tf_op jit(solution)/shard_map/ppermute | solution.py:437
  31.0 1.9 collective-permute-start
  32.9 18.6 %collective-permute-done.2.refs_3_ = bf16[128,4224]{1,0:T(8,128)(2,1)S(1)} collective-permute-done((bf16[128,4224]{1,0:T(8,128)(2,1)S(1)}, bf16[128,4224]{1,0:T(8,128)(2,1)S(1)}, u32[]{:S(2)}, u32[]{:S(2)}) %collective-permute-start.2) | collective-permute-done | bytes 1081376 | tf_op jit(solution)/shard_map/ppermute | solution.py:437
  51.5 0.0 copy-start.1
  51.5 3.4 %collective-permute-done.1.refs_2_ = bf16[128,4224]{1,0:T(8,128)(2,1)S(1)} collective-permute-done((bf16[128,4224]{1,0:T(8,128)(2,1)S(1)}, bf16[128,4224]{1,0:T(8,128)(2,1)S(1)}, u32[]{:S(2)}, u32[]{:S(2)}) %collective-permute-start.1) | collective-permute-done | bytes 1081376 | tf_op jit(solution)/shard_map/ppermute | solution.py:437
  54.9 0.0 copy-start.2
  54.9 24.1 %collective-permute-done.refs_1_ = bf16[128,4224]{1,0:T(8,128)(2,1)} collective-permute-done((bf16[128,4224]{1,0:T(8,128)(2,1)S(1)}, bf16[128,4224]{1,0:T(8,128)(2,1)}, u32[]{:S(2)}, u32[]{:S(2)}) %collective-permute-start) | collective-permute-done | bytes 1081376 | tf_op jit(solution)/shard_map/ppermute | solution.py:437
  79.0 0.0 copy-done
  79.1 0.0 copy-done.1
  79.1 0.0 copy-done.2
  79.1 10.2 %shard_map.146 = (s32[3,128]{1,0:T(4,128)}, bf16[512,2048]{1,0:T(8,128)(2,1)}, bf16[512,2048]{1,0:T(8,128)(2,1)}, bf16[2048,512]{1,0:T(8,128)(2,1)}, bf16[2048,5...) custom-call(s32[3,128]{1,0:T(4,128)} %bitcast.5, bf16[128,4224]{1,0:T(8,128)(2,1)} %copy-done, ...), custom_call_target="tpu_custom_call" | custom-call | bytes 12848128 | tf_op jit(solution)/shard_map/pallas_call | solution.py:301
  89.3 21.5 %all-to-all-done = bf16[128,16,896]{2,1,0:T(8,128)(2,1)} async-done(((bf16[128,16,896]{2,1,0:T(8,128)(2,1)}), bf16[128,16,896]{2,1,0:T(8,128)(2,1)}, u32[]{:S(2)}, u32[]{:S(2)}) %all-to-all-start) | async-done | bytes 3670048 | tf_op jit(solution)/shard_map/all_to_all | solution.py:433
  110.7 10.4 %shard_map.148 = (bf16[2048,896]{1,0:T(8,128)(2,1)}, bf16[512,1024]{1,0:T(8,128)(2,1)}) custom-call(bf16[512,2048]{1,0:T(8,128)(2,1)} %get-tuple-element.20.x_hbm, bf16[512,2048]{1,0:T(8,128)(2,1)} %get-tuple-element.21.dy_hbm, bf16[2048,512]{1,0:T(8,128)(2,1)} %get-tuple-element.22.xt_hbm, bf16[2048,512]{1,0:T(8,128)(2,1)} %get-tuple-element.23.dyt_hbm, ...), custom_call_target="tpu_custom_call" | custom-call | flops 3623878656 | bytes 16908288 | tf_op jit(solution)/shard_map/pallas_call | solution.py:301
  121.1 8.5 %all-to-all-start.1 = ((bf16[128,16,896]{2,1,0:T(8,128)(2,1)}), bf16[128,16,896]{2,1,0:T(8,128)(2,1)}, u32[]{:S(2)}, u32[]{:S(2)}) async-start(bf16[128,16,896]{2,1,0:T(8,128)(2,1)} %bitcast.3), calls=%async_computation.1 | async-start | bytes 7340032 | tf_op jit(solution)/shard_map/all_to_all | solution.py:443
  129.6 7.8 %shard_map.149 = (bf16[128,4096]{1,0:T(8,128)(2,1)}, bf16[128,4096]{1,0:T(8,128)(2,1)}, bf16[128,4096]{1,0:T(8,128)(2,1)}, bf16[128,4096]{1,0:T(8,128)(2,1)}) custom-call(bf16[512,1024]{1,0:T(8,128)(2,1)} %get-tuple-element.25.act_ref, bf16[2048,896]{1,0:T(8,128)(2,1)} %bitcast.1.w_hbm.w_ref), custom_call_target="tpu_custom_call" | custom-call | flops 1811939328 | bytes 8912896 | tf_op jit(solution)/shard_map/pallas_call | solution.py:301
  137.3 2.1 collective-permute-start.3
  139.5 4.4 %collective-permute-start.4 = (bf16[128,4096]{1,0:T(8,128)(2,1)}, bf16[128,4096]{1,0:T(8,128)(2,1)S(1)}, u32[]{:S(2)}, u32[]{:S(2)}) collective-permute-start(bf16[128,4096]{1,0:T(8,128)(2,1)} %get-tuple-element.28), channel_id=1, source_target_pairs={{0,2},{1,3},{2,0},{3,1},{4,6},{5,7},{6,4},{7,5},{8,10},{9,11},{10,... | collective-permute-start | bytes 3145736 | tf_op jit(solution)/shard_map/ppermute | solution.py:437
  143.9 1.9 collective-permute-start.5
  145.8 18.1 %collective-permute-done.3 = bf16[128,4096]{1,0:T(8,128)(2,1)S(1)} collective-permute-done((bf16[128,4096]{1,0:T(8,128)(2,1)}, bf16[128,4096]{1,0:T(8,128)(2,1)S(1)}, u32[]{:S(2)}, u32[]{:S(2)}) %collective-permute-start.3) | collective-permute-done | bytes 1048608 | tf_op jit(solution)/shard_map/ppermute | solution.py:437
  163.9 3.4 %collective-permute-done.4 = bf16[128,4096]{1,0:T(8,128)(2,1)S(1)} collective-permute-done((bf16[128,4096]{1,0:T(8,128)(2,1)}, bf16[128,4096]{1,0:T(8,128)(2,1)S(1)}, u32[]{:S(2)}, u32[]{:S(2)}) %collective-permute-start.4) | collective-permute-done | bytes 1048608 | tf_op jit(solution)/shard_map/ppermute | solution.py:437
  167.3 23.4 %collective-permute-done.5 = bf16[128,4096]{1,0:T(8,128)(2,1)S(1)} collective-permute-done((bf16[128,4096]{1,0:T(8,128)(2,1)}, bf16[128,4096]{1,0:T(8,128)(2,1)S(1)}, u32[]{:S(2)}, u32[]{:S(2)}) %collective-permute-start.5) | collective-permute-done | bytes 1048608 | tf_op jit(solution)/shard_map/ppermute | solution.py:437
  190.8 1.9 add_convert_fusion
  192.6 1.0 fusion
  193.7 22.5 %all-to-all-done.1.recv_ref = bf16[128,16,896]{2,1,0:T(8,128)(2,1)} async-done(((bf16[128,16,896]{2,1,0:T(8,128)(2,1)}), bf16[128,16,896]{2,1,0:T(8,128)(2,1)}, u32[]{:S(2)}, u32[]{:S(2)}) %all-to-all-start.1) | async-done | bytes 3670048 | tf_op jit(solution)/shard_map/all_to_all | solution.py:443
  216.2 6.3 %shard_map.150 = (bf16[16,96,128]{2,1,0:T(8,128)(2,1)}, bf16[16,96,128]{2,1,0:T(8,128)(2,1)}, bf16[16,96,128]{2,1,0:T(8,128)(2,1)}) custom-call(s32[3,128]{1,0:T(4,128)} %get-tuple-element.30.places_ref, bf16[128,16,896]{2,1,0:T(8,128)(2,1)} %all-to-all-done.1.recv_ref), custom_call_target="tpu_custom_call" | custom-call | bytes 4851200 | tf_op jit(solution)/shard_map/pallas_call | solution.py:301
  (2 shorter events, 0.0 us)
Async XLA Ops:
  5.9 18.3 %copy-start.6 = (s32[128,2]{0,1:T(2,128)S(1)}, s32[128,2]{0,1:T(2,128)}, u32[]{:S(2)}) copy-start(s32[128,2]{0,1:T(2,128)} %param.13) | copy-start | bytes 3076
  5.9 18.3 %copy-start.5 = (s32[128,2]{0,1:T(2,128)S(1)}, s32[128,2]{0,1:T(2,128)}, u32[]{:S(2)}) copy-start(s32[128,2]{0,1:T(2,128)} %param.12) | copy-start | bytes 3076
  5.9 18.4 %copy-start.3 = (bf16[128,2048]{1,0:T(8,128)(2,1)S(1)}, bf16[128,2048]{1,0:T(8,128)(2,1)}, u32[]{:S(2)}) copy-start(bf16[128,2048]{1,0:T(8,128)(2,1)} %param.21) | copy-start | bytes 1572868
  5.9 18.4 %copy-start.4 = (bf16[128,2048]{1,0:T(8,128)(2,1)S(1)}, bf16[128,2048]{1,0:T(8,128)(2,1)}, u32[]{:S(2)}) copy-start(bf16[128,2048]{1,0:T(8,128)(2,1)} %param.11) | copy-start | bytes 1572868
  5.9 104.8 %all-to-all-start = ((bf16[128,16,896]{2,1,0:T(8,128)(2,1)}), bf16[128,16,896]{2,1,0:T(8,128)(2,1)}, u32[]{:S(2)}, u32[]{:S(2)}) async-start(bf16[128,16,896]{2,1,0:T(8,128)(2,1)} %shard_map.147), calls=%async_computation | async-start | bytes 7340032 | tf_op jit(solution)/shard_map/all_to_all | solution.py:433
  24.4 54.6 %copy-start = (bf16[128,4224]{1,0:T(8,128)(2,1)}, bf16[128,4224]{1,0:T(8,128)(2,1)S(1)}, u32[]{:S(2)}) copy-start(bf16[128,4224]{1,0:T(8,128)(2,1)S(1)} %pad_maximum_fusion.refs_0_) | copy-start | bytes 3244036
  24.4 27.1 %collective-permute-start.2 = (bf16[128,4224]{1,0:T(8,128)(2,1)S(1)}, bf16[128,4224]{1,0:T(8,128)(2,1)S(1)}, u32[]{:S(2)}, u32[]{:S(2)}) collective-permute-start(bf16[128,4224]{1,0:T(8,128)(2,1)S(1)} %pad_maximum_fusion.refs_0_), channel_id=1, source_target_pairs={{0,3},{1,0},{2,1},{3,2},{4,7},{5,4},{6,5},{7,6},{8,11},{9,8},{10,9... | collective-permute-start | bytes 3244040 | tf_op jit(solution)/shard_map/ppermute | solution.py:437
  26.6 28.3 %collective-permute-start.1 = (bf16[128,4224]{1,0:T(8,128)(2,1)S(1)}, bf16[128,4224]{1,0:T(8,128)(2,1)S(1)}, u32[]{:S(2)}, u32[]{:S(2)}) collective-permute-start(bf16[128,4224]{1,0:T(8,128)(2,1)S(1)} %pad_maximum_fusion.refs_0_), channel_id=1, source_target_pairs={{0,2},{1,3},{2,0},{3,1},{4,6},{5,7},{6,4},{7,5},{8,10},{9,11},{10,... | collective-permute-start | bytes 3244040 | tf_op jit(solution)/shard_map/ppermute | solution.py:437
  31.0 48.1 %collective-permute-start = (bf16[128,4224]{1,0:T(8,128)(2,1)S(1)}, bf16[128,4224]{1,0:T(8,128)(2,1)}, u32[]{:S(2)}, u32[]{:S(2)}) collective-permute-start(bf16[128,4224]{1,0:T(8,128)(2,1)S(1)} %pad_maximum_fusion.refs_0_), channel_id=1, source_target_pairs={{0,1},{1,2},{2,3},{3,0},{4,5},{5,6},{6,7},{7,4},{8,9},{9,10},{10,1... | collective-permute-start | bytes 3244040 | tf_op jit(solution)/shard_map/ppermute | solution.py:437
  51.5 27.5 %copy-start.1 = (bf16[128,4224]{1,0:T(8,128)(2,1)}, bf16[128,4224]{1,0:T(8,128)(2,1)S(1)}, u32[]{:S(2)}) copy-start(bf16[128,4224]{1,0:T(8,128)(2,1)S(1)} %collective-permute-done.2.refs_3_) | copy-start | bytes 3244036
  54.9 24.2 %copy-start.2 = (bf16[128,4224]{1,0:T(8,128)(2,1)}, bf16[128,4224]{1,0:T(8,128)(2,1)S(1)}, u32[]{:S(2)}) copy-start(bf16[128,4224]{1,0:T(8,128)(2,1)S(1)} %collective-permute-done.1.refs_2_) | copy-start | bytes 3244036
  121.1 95.1 %all-to-all-start.1 = ((bf16[128,16,896]{2,1,0:T(8,128)(2,1)}), bf16[128,16,896]{2,1,0:T(8,128)(2,1)}, u32[]{:S(2)}, u32[]{:S(2)}) async-start(bf16[128,16,896]{2,1,0:T(8,128)(2,1)} %bitcast.3), calls=%async_computation.1 | async-start | bytes 7340032 | tf_op jit(solution)/shard_map/all_to_all | solution.py:443
  137.3 26.6 %collective-permute-start.3 = (bf16[128,4096]{1,0:T(8,128)(2,1)}, bf16[128,4096]{1,0:T(8,128)(2,1)S(1)}, u32[]{:S(2)}, u32[]{:S(2)}) collective-permute-start(bf16[128,4096]{1,0:T(8,128)(2,1)} %get-tuple-element.27), channel_id=1, source_target_pairs={{0,3},{1,0},{2,1},{3,2},{4,7},{5,4},{6,5},{7,6},{8,11},{9,8},{10,9... | collective-permute-start | bytes 3145736 | tf_op jit(solution)/shard_map/ppermute | solution.py:437
  139.5 27.8 %collective-permute-start.4 = (bf16[128,4096]{1,0:T(8,128)(2,1)}, bf16[128,4096]{1,0:T(8,128)(2,1)S(1)}, u32[]{:S(2)}, u32[]{:S(2)}) collective-permute-start(bf16[128,4096]{1,0:T(8,128)(2,1)} %get-tuple-element.28), channel_id=1, source_target_pairs={{0,2},{1,3},{2,0},{3,1},{4,6},{5,7},{6,4},{7,5},{8,10},{9,11},{10,... | collective-permute-start | bytes 3145736 | tf_op jit(solution)/shard_map/ppermute | solution.py:437
  143.9 46.9 %collective-permute-start.5 = (bf16[128,4096]{1,0:T(8,128)(2,1)}, bf16[128,4096]{1,0:T(8,128)(2,1)S(1)}, u32[]{:S(2)}, u32[]{:S(2)}) collective-permute-start(bf16[128,4096]{1,0:T(8,128)(2,1)} %get-tuple-element.29), channel_id=1, source_target_pairs={{0,1},{1,2},{2,3},{3,0},{4,5},{5,6},{6,7},{7,4},{8,9},{9,10},{10,1... | collective-permute-start | bytes 3145736 | tf_op jit(solution)/shard_map/ppermute | solution.py:437

commit v3 on v2

--- a/solution.py
+++ b/solution.py
@@ -29,20 +29,36 @@
 
 
 def pack_kernel(
-    hits_ref, gate_hbm, up_hbm, down_hbm, gs_ref, us_ref, ds_ref, out_ref, stored, held, wide, ready, in_sem, sem
+    hits_hbm,
+    gate_hbm,
+    up_hbm,
+    down_hbm,
+    gs_hbm,
+    us_hbm,
+    ds_hbm,
+    out_ref,
+    hits_ref,
+    stored,
+    scales,
+    held,
+    wide,
+    ready,
+    in_sem,
+    sem,
 ):
     _, rows, block, experts = stored.shape
     groups = out_ref.shape[0]
-    fetches = [
-        pltpu.make_async_copy(w_hbm, stored.at[m], in_sem.at[m])
-        for m, w_hbm in enumerate((gate_hbm, up_hbm, down_hbm))
-    ]
+    pairs = [(hits_hbm, hits_ref)]
+    for m, (w_hbm, s_hbm) in enumerate(((gate_hbm, gs_hbm), (up_hbm, us_hbm), (down_hbm, ds_hbm))):
+        pairs += [(s_hbm, scales.at[m]), (w_hbm, stored.at[m])]
+    fetches = [pltpu.make_async_copy(*pair, in_sem.at[i]) for i, pair in enumerate(pairs)]
     for copy in fetches:
         copy.start()
-    for m, s_ref in enumerate((gs_ref, us_ref, ds_ref)):
-        wide[m] = s_ref[...].astype(jnp.float32)
+    fetches[0].wait()
     for m in range(3):
-        fetches[m].wait()
+        fetches[2 * m + 1].wait()
+        fetches[2 * m + 2].wait()
+        wide[m] = scales[m].astype(jnp.float32)
 
         def scaled(r, m=m):
             w = (stored[m, r].astype(jnp.float32) * wide[m, pl.ds(r, 1), :]).astype(jnp.bfloat16)
@@ -85,8 +101,10 @@
         move(i).wait()
 
 
-def settle_kernel(places_ref, recv_ref, gate_ref, up_ref, down_ref, here, norm, acc, sem):
-    rows, block, experts = gate_ref.shape
+def settle_kernel(
+    places_hbm, recv_ref, gate_ref, up_ref, down_ref, places_ref, here, norm, acc, grads, sem, places_sem, out_sem
+):
+    _, rows, block, experts = grads.shape
     groups = recv_ref.shape[0]
     size = groups // PARTS
 
@@ -96,6 +114,8 @@
 
     for i in range(PARTS):
         move(i).start()
+    get_places = pltpu.make_async_copy(places_hbm, places_ref, places_sem)
+    get_places.start()
     lane = lane_index((rows, LANES))
 
     def terms(g):
@@ -134,17 +154,25 @@
         for m in range(3):
             acc[m, pl.ds(pl.multiple_of(e * rows, rows), rows), :] = out[m]
 
+    get_places.wait()
     batched(experts, 16, total, put)
-    refs = (gate_ref, up_ref, down_ref)
 
     def flipped(r):
         return [acc[m, pl.ds(r, experts, stride=rows), :].astype(jnp.bfloat16).T[:block] for m in range(3)]
 
     def finish(r, out):
         for m in range(3):
-            refs[m][r] = out[m]
-
-    batched(rows, 8, flipped, finish)
+            grads[m, r] = out[m]
+
+    puts = []
+    for half in range(2):
+        part = pl.ds(half * rows // 2, rows // 2)
+        batched(rows // 2, 8, lambda r, h=half: flipped(h * rows // 2 + r), lambda r, out, h=half: finish(h * rows // 2 + r, out))
+        for m, ref in enumerate((gate_ref, up_ref, down_ref)):
+            puts.append(pltpu.make_async_copy(grads.at[m, part], ref.at[part], out_sem.at[3 * half + m]))
+            puts[-1].start()
+    for copy in puts:
+        copy.wait()
 
 
 def dot(left, right):
@@ -208,9 +236,8 @@
     chunk = CHUNK
     lane = lane_index((chunk, LANES))
 
-    @pl.loop(0, tok // chunk)
-    def _(i):
-        rows = pl.ds(pl.multiple_of(i * chunk, chunk), chunk)
+    for i in range(tok // chunk):
+        rows = pl.ds(i * chunk, chunk)
         share = rw[rows, :].astype(jnp.float32)
         one, two, three = share[:, 0:1], share[:, 1:2], share[:, 2:3]
         for h, part in enumerate((jnp.where(lane < 96, one, two), jnp.where(lane < 64, two, three))):
@@ -320,18 +347,20 @@
     rows, _, experts = weights[0].shape
     groups = hits.shape[1]
     scratch = (
+        SMEM(hits.shape, jnp.int32),
         VMEM((3, *weights[0].shape), jnp.bfloat16),
+        VMEM((3, rows, experts), jnp.bfloat16),
         VMEM((3, rows * experts, LANES), jnp.float32),
         VMEM((3, rows, experts), jnp.float32),
         VMEM((groups, rows, COLUMNS), jnp.bfloat16),
-        pltpu.SemaphoreType.DMA((3,)),
+        pltpu.SemaphoreType.DMA((7,)),
         pltpu.SemaphoreType.DMA((PARTS,)),
     )
     return call(
         pack_kernel,
         [shape(groups, rows, COLUMNS)],
         (hits, *weights, *scales),
-        [SMEM] + [ANY] * 3 + [VMEM] * 3,
+        [ANY] * 7,
         [ANY],
         scratch,
         limit=60,
@@ -342,13 +371,17 @@
     rows, _, experts = like.shape
     groups = received.shape[0]
     scratch = (
+        SMEM(places.shape, jnp.int32),
         VMEM((groups, rows, COLUMNS), jnp.bfloat16),
         VMEM((3, 3 * groups, rows, LANES), jnp.bfloat16),
         VMEM((3, experts * rows, LANES), jnp.float32),
+        VMEM((3, *like.shape), jnp.bfloat16),
         pltpu.SemaphoreType.DMA((PARTS,)),
+        pltpu.SemaphoreType.DMA,
+        pltpu.SemaphoreType.DMA((6,)),
     )
     return call(
-        settle_kernel, [shape(*like.shape)] * 3, (places, received), [SMEM, ANY], [VMEM] * 3, scratch, limit=60
+        settle_kernel, [shape(*like.shape)] * 3, (places, received), [ANY] * 2, [ANY] * 3, scratch, limit=60
     )
 
 

time: 223 us -> 222 us (level)
  no operation moved by 1% of the time
where the time goes in v3:
time: 222 us; the launch traced here: 221 us
  waiting for transfers between devices  135 us (61%)
  starting transfers between devices  43.7 us (20%)
  Pallas kernels  38.3 us (17%)
    ppermute x6, waiting for transfers between devices, shift(): lax.ppermute(value, 'narrow', [(i, (i + step) % devices) for i in range(d...  91.1 us
    pallas_call x5, Pallas kernels, call(): pl.pallas_call(body, out_shape=outputs, in_specs=[pl.BlockSpec(memory_spa...  38.3 us
    all_to_all x1, waiting for transfers between devices, per_device(): lax.all_to_all(terms.reshape(groups, owner_rows, COLUMNS), 'wide', split_...  22.5 us
    all_to_all x1, waiting for transfers between devices, per_device(): lax.all_to_all(sent, 'wide', split_axis=0, concat_axis=0, tiled=True)  21.5 us
    all_to_all x1, starting transfers between devices, per_device(): lax.all_to_all(sent, 'wide', split_axis=0, concat_axis=0, tiled=True)  18.2 us
    ppermute x6, starting transfers between devices, shift(): lax.ppermute(value, 'narrow', [(i, (i + step) % devices) for i in range(d...  16.9 us
    all_to_all x1, starting transfers between devices, per_device(): lax.all_to_all(terms.reshape(groups, owner_rows, COLUMNS), 'wide', split_...  8.65 us
  transfers between devices with their start and end apart: 8, of which 8 were waited for; matrix products, arithmetic and copies ran while one was open for 1% of the time, Pallas kernels for 8%

profile of v3, /device:TPU:29, one launch (start us, length us, event | category | flops | bytes accessed | tf_op | source)
XLA Modules:
  0.0 221.3 jit_solution(12298646527487810166)
XLA Ops:
  0.6 4.5 %shard_map.147 = bf16[128,16,896]{2,1,0:T(8,128)(2,1)} custom-call(s32[3,128]{1,0:T(4,128)} %bitcast.4, bf16[16,96,128]{2,1,0:T(8,128)(2,1)} %gate_hbm.1, bf16[16,96,128]{2,1,0:T(8,128)(2,1)} %up_hbm.1, bf16[16,96,128]{2,1,0:T(8,128)(2,1)} %down_hbm.1, bf16[16,128]{1,0:T(8,128)(2,1)} %gs_hbm.1, bf16[16,128]{1,0:T(8,128)(2,1)} %us_hbm.1, bf16[16,128]{1,0:T(8,128)(2,1)} %ds_hbm.1), custom_call_target="tpu_custom_call" | custom-call | bytes 4863488 | tf_op jit(solution)/shard_map/pallas_call | solution.py:328
  5.1 0.0 copy-start.6
  5.1 0.0 copy-start.5
  5.1 0.0 copy-start.3
  5.2 0.0 copy-start.4
  5.2 18.2 %all-to-all-start = ((bf16[128,16,896]{2,1,0:T(8,128)(2,1)}), bf16[128,16,896]{2,1,0:T(8,128)(2,1)}, u32[]{:S(2)}, u32[]{:S(2)}) async-start(bf16[128,16,896]{2,1,0:T(8,128)(2,1)} %shard_map.147), calls=%async_computation | async-start | bytes 7340032 | tf_op jit(solution)/shard_map/all_to_all | solution.py:466
  23.4 0.0 copy-done.6
  23.4 0.0 copy-done.5
  23.4 0.1 select_reduce_fusion
  23.6 0.0 copy-done.3
  23.6 0.0 copy-done.4
  23.6 0.1 pad_maximum_fusion.refs_0_
  23.7 0.0 copy-start
  23.7 2.2 collective-permute-start.2
  25.9 4.4 %collective-permute-start.1 = (bf16[128,4224]{1,0:T(8,128)(2,1)S(1)}, bf16[128,4224]{1,0:T(8,128)(2,1)S(1)}, u32[]{:S(2)}, u32[]{:S(2)}) collective-permute-start(bf16[128,4224]{1,0:T(8,128)(2,1)S(1)} %pad_maximum_fusion.refs_0_), channel_id=1, source_target_pairs={{0,2},{1,3},{2,0},{3,1},{4,6},{5,7},{6,4},{7,5},{8,10},{9,11},{10,... | collective-permute-start | bytes 3244040 | tf_op jit(solution)/shard_map/ppermute | solution.py:470
  30.2 1.9 collective-permute-start
  32.2 18.6 %collective-permute-done.2.refs_3_ = bf16[128,4224]{1,0:T(8,128)(2,1)S(1)} collective-permute-done((bf16[128,4224]{1,0:T(8,128)(2,1)S(1)}, bf16[128,4224]{1,0:T(8,128)(2,1)S(1)}, u32[]{:S(2)}, u32[]{:S(2)}) %collective-permute-start.2) | collective-permute-done | bytes 1081376 | tf_op jit(solution)/shard_map/ppermute | solution.py:470
  50.8 0.0 copy-start.1
  50.8 3.4 %collective-permute-done.1.refs_2_ = bf16[128,4224]{1,0:T(8,128)(2,1)S(1)} collective-permute-done((bf16[128,4224]{1,0:T(8,128)(2,1)S(1)}, bf16[128,4224]{1,0:T(8,128)(2,1)S(1)}, u32[]{:S(2)}, u32[]{:S(2)}) %collective-permute-start.1) | collective-permute-done | bytes 1081376 | tf_op jit(solution)/shard_map/ppermute | solution.py:470
  54.2 0.0 copy-start.2
  54.2 24.1 %collective-permute-done.refs_1_ = bf16[128,4224]{1,0:T(8,128)(2,1)} collective-permute-done((bf16[128,4224]{1,0:T(8,128)(2,1)S(1)}, bf16[128,4224]{1,0:T(8,128)(2,1)}, u32[]{:S(2)}, u32[]{:S(2)}) %collective-permute-start) | collective-permute-done | bytes 1081376 | tf_op jit(solution)/shard_map/ppermute | solution.py:470
  78.3 0.0 copy-done
  78.3 0.0 copy-done.1
  78.3 0.0 copy-done.2
  78.3 10.2 %shard_map.146 = (s32[3,128]{1,0:T(4,128)}, bf16[512,2048]{1,0:T(8,128)(2,1)}, bf16[512,2048]{1,0:T(8,128)(2,1)}, bf16[2048,512]{1,0:T(8,128)(2,1)}, bf16[2048,5...) custom-call(s32[3,128]{1,0:T(4,128)} %bitcast.5, bf16[128,4224]{1,0:T(8,128)(2,1)} %copy-done, ...), custom_call_target="tpu_custom_call" | custom-call | bytes 12848128 | tf_op jit(solution)/shard_map/pallas_call | solution.py:328
  88.5 21.5 %all-to-all-done = bf16[128,16,896]{2,1,0:T(8,128)(2,1)} async-done(((bf16[128,16,896]{2,1,0:T(8,128)(2,1)}), bf16[128,16,896]{2,1,0:T(8,128)(2,1)}, u32[]{:S(2)}, u32[]{:S(2)}) %all-to-all-start) | async-done | bytes 3670048 | tf_op jit(solution)/shard_map/all_to_all | solution.py:466
  110.0 10.3 %shard_map.148 = (bf16[2048,896]{1,0:T(8,128)(2,1)}, bf16[512,1024]{1,0:T(8,128)(2,1)}) custom-call(bf16[512,2048]{1,0:T(8,128)(2,1)} %get-tuple-element.20.x_hbm, bf16[512,2048]{1,0:T(8,128)(2,1)} %get-tuple-element.21.dy_hbm, bf16[2048,512]{1,0:T(8,128)(2,1)} %get-tuple-element.22.xt_hbm, bf16[2048,512]{1,0:T(8,128)(2,1)} %get-tuple-element.23.dyt_hbm, ...), custom_call_target="tpu_custom_call" | custom-call | flops 3623878656 | bytes 16908288 | tf_op jit(solution)/shard_map/pallas_call | solution.py:328
  120.3 8.6 %all-to-all-start.1 = ((bf16[128,16,896]{2,1,0:T(8,128)(2,1)}), bf16[128,16,896]{2,1,0:T(8,128)(2,1)}, u32[]{:S(2)}, u32[]{:S(2)}) async-start(bf16[128,16,896]{2,1,0:T(8,128)(2,1)} %bitcast.3), calls=%async_computation.1 | async-start | bytes 7340032 | tf_op jit(solution)/shard_map/all_to_all | solution.py:476
  129.0 7.7 %shard_map.149 = (bf16[128,4096]{1,0:T(8,128)(2,1)}, bf16[128,4096]{1,0:T(8,128)(2,1)}, bf16[128,4096]{1,0:T(8,128)(2,1)}, bf16[128,4096]{1,0:T(8,128)(2,1)}) custom-call(bf16[512,1024]{1,0:T(8,128)(2,1)} %get-tuple-element.25.act_ref, bf16[2048,896]{1,0:T(8,128)(2,1)} %bitcast.1.w_hbm.w_ref), custom_call_target="tpu_custom_call" | custom-call | flops 1811939328 | bytes 8912896 | tf_op jit(solution)/shard_map/pallas_call | solution.py:328
  136.7 2.1 collective-permute-start.3
  138.9 4.4 %collective-permute-start.4 = (bf16[128,4096]{1,0:T(8,128)(2,1)}, bf16[128,4096]{1,0:T(8,128)(2,1)S(1)}, u32[]{:S(2)}, u32[]{:S(2)}) collective-permute-start(bf16[128,4096]{1,0:T(8,128)(2,1)} %get-tuple-element.28), channel_id=1, source_target_pairs={{0,2},{1,3},{2,0},{3,1},{4,6},{5,7},{6,4},{7,5},{8,10},{9,11},{10,... | collective-permute-start | bytes 3145736 | tf_op jit(solution)/shard_map/ppermute | solution.py:470
  143.3 1.9 collective-permute-start.5
  145.2 18.1 %collective-permute-done.3 = bf16[128,4096]{1,0:T(8,128)(2,1)S(1)} collective-permute-done((bf16[128,4096]{1,0:T(8,128)(2,1)}, bf16[128,4096]{1,0:T(8,128)(2,1)S(1)}, u32[]{:S(2)}, u32[]{:S(2)}) %collective-permute-start.3) | collective-permute-done | bytes 1048608 | tf_op jit(solution)/shard_map/ppermute | solution.py:470
  163.3 3.4 %collective-permute-done.4 = bf16[128,4096]{1,0:T(8,128)(2,1)S(1)} collective-permute-done((bf16[128,4096]{1,0:T(8,128)(2,1)}, bf16[128,4096]{1,0:T(8,128)(2,1)S(1)}, u32[]{:S(2)}, u32[]{:S(2)}) %collective-permute-start.4) | collective-permute-done | bytes 1048608 | tf_op jit(solution)/shard_map/ppermute | solution.py:470
  166.7 23.4 %collective-permute-done.5 = bf16[128,4096]{1,0:T(8,128)(2,1)S(1)} collective-permute-done((bf16[128,4096]{1,0:T(8,128)(2,1)}, bf16[128,4096]{1,0:T(8,128)(2,1)S(1)}, u32[]{:S(2)}, u32[]{:S(2)}) %collective-permute-start.5) | collective-permute-done | bytes 1048608 | tf_op jit(solution)/shard_map/ppermute | solution.py:470
  190.2 1.9 add_convert_fusion
  192.0 1.0 fusion
  193.1 22.5 %all-to-all-done.1.recv_ref = bf16[128,16,896]{2,1,0:T(8,128)(2,1)} async-done(((bf16[128,16,896]{2,1,0:T(8,128)(2,1)}), bf16[128,16,896]{2,1,0:T(8,128)(2,1)}, u32[]{:S(2)}, u32[]{:S(2)}) %all-to-all-start.1) | async-done | bytes 3670048 | tf_op jit(solution)/shard_map/all_to_all | solution.py:476
  215.6 5.5 %shard_map.150 = (bf16[16,96,128]{2,1,0:T(8,128)(2,1)}, bf16[16,96,128]{2,1,0:T(8,128)(2,1)}, bf16[16,96,128]{2,1,0:T(8,128)(2,1)}) custom-call(s32[3,128]{1,0:T(4,128)} %get-tuple-element.30.places_hbm, bf16[128,16,896]{2,1,0:T(8,128)(2,1)} %all-to-all-done.1.recv_ref), custom_call_target="tpu_custom_call" | custom-call | bytes 4851200 | tf_op jit(solution)/shard_map/pallas_call | solution.py:328
  (2 shorter events, 0.0 us)
Async XLA Ops:
  5.1 18.3 %copy-start.6 = (s32[128,2]{0,1:T(2,128)S(1)}, s32[128,2]{0,1:T(2,128)}, u32[]{:S(2)}) copy-start(s32[128,2]{0,1:T(2,128)} %param.13) | copy-start | bytes 3076
  5.1 18.3 %copy-start.5 = (s32[128,2]{0,1:T(2,128)S(1)}, s32[128,2]{0,1:T(2,128)}, u32[]{:S(2)}) copy-start(s32[128,2]{0,1:T(2,128)} %param.12) | copy-start | bytes 3076
  5.1 18.4 %copy-start.3 = (bf16[128,2048]{1,0:T(8,128)(2,1)S(1)}, bf16[128,2048]{1,0:T(8,128)(2,1)}, u32[]{:S(2)}) copy-start(bf16[128,2048]{1,0:T(8,128)(2,1)} %param.21) | copy-start | bytes 1572868
  5.2 18.4 %copy-start.4 = (bf16[128,2048]{1,0:T(8,128)(2,1)S(1)}, bf16[128,2048]{1,0:T(8,128)(2,1)}, u32[]{:S(2)}) copy-start(bf16[128,2048]{1,0:T(8,128)(2,1)} %param.11) | copy-start | bytes 1572868
  5.2 104.8 %all-to-all-start = ((bf16[128,16,896]{2,1,0:T(8,128)(2,1)}), bf16[128,16,896]{2,1,0:T(8,128)(2,1)}, u32[]{:S(2)}, u32[]{:S(2)}) async-start(bf16[128,16,896]{2,1,0:T(8,128)(2,1)} %shard_map.147), calls=%async_computation | async-start | bytes 7340032 | tf_op jit(solution)/shard_map/all_to_all | solution.py:466
  23.7 54.6 %copy-start = (bf16[128,4224]{1,0:T(8,128)(2,1)}, bf16[128,4224]{1,0:T(8,128)(2,1)S(1)}, u32[]{:S(2)}) copy-start(bf16[128,4224]{1,0:T(8,128)(2,1)S(1)} %pad_maximum_fusion.refs_0_) | copy-start | bytes 3244036
  23.7 27.1 %collective-permute-start.2 = (bf16[128,4224]{1,0:T(8,128)(2,1)S(1)}, bf16[128,4224]{1,0:T(8,128)(2,1)S(1)}, u32[]{:S(2)}, u32[]{:S(2)}) collective-permute-start(bf16[128,4224]{1,0:T(8,128)(2,1)S(1)} %pad_maximum_fusion.refs_0_), channel_id=1, source_target_pairs={{0,3},{1,0},{2,1},{3,2},{4,7},{5,4},{6,5},{7,6},{8,11},{9,8},{10,9... | collective-permute-start | bytes 3244040 | tf_op jit(solution)/shard_map/ppermute | solution.py:470
  25.9 28.3 %collective-permute-start.1 = (bf16[128,4224]{1,0:T(8,128)(2,1)S(1)}, bf16[128,4224]{1,0:T(8,128)(2,1)S(1)}, u32[]{:S(2)}, u32[]{:S(2)}) collective-permute-start(bf16[128,4224]{1,0:T(8,128)(2,1)S(1)} %pad_maximum_fusion.refs_0_), channel_id=1, source_target_pairs={{0,2},{1,3},{2,0},{3,1},{4,6},{5,7},{6,4},{7,5},{8,10},{9,11},{10,... | collective-permute-start | bytes 3244040 | tf_op jit(solution)/shard_map/ppermute | solution.py:470
  30.2 48.1 %collective-permute-start = (bf16[128,4224]{1,0:T(8,128)(2,1)S(1)}, bf16[128,4224]{1,0:T(8,128)(2,1)}, u32[]{:S(2)}, u32[]{:S(2)}) collective-permute-start(bf16[128,4224]{1,0:T(8,128)(2,1)S(1)} %pad_maximum_fusion.refs_0_), channel_id=1, source_target_pairs={{0,1},{1,2},{2,3},{3,0},{4,5},{5,6},{6,7},{7,4},{8,9},{9,10},{10,1... | collective-permute-start | bytes 3244040 | tf_op jit(solution)/shard_map/ppermute | solution.py:470
  50.8 27.5 %copy-start.1 = (bf16[128,4224]{1,0:T(8,128)(2,1)}, bf16[128,4224]{1,0:T(8,128)(2,1)S(1)}, u32[]{:S(2)}) copy-start(bf16[128,4224]{1,0:T(8,128)(2,1)S(1)} %collective-permute-done.2.refs_3_) | copy-start | bytes 3244036
  54.2 24.2 %copy-start.2 = (bf16[128,4224]{1,0:T(8,128)(2,1)}, bf16[128,4224]{1,0:T(8,128)(2,1)S(1)}, u32[]{:S(2)}) copy-start(bf16[128,4224]{1,0:T(8,128)(2,1)S(1)} %collective-permute-done.1.refs_2_) | copy-start | bytes 3244036
  120.3 95.3 %all-to-all-start.1 = ((bf16[128,16,896]{2,1,0:T(8,128)(2,1)}), bf16[128,16,896]{2,1,0:T(8,128)(2,1)}, u32[]{:S(2)}, u32[]{:S(2)}) async-start(bf16[128,16,896]{2,1,0:T(8,128)(2,1)} %bitcast.3), calls=%async_computation.1 | async-start | bytes 7340032 | tf_op jit(solution)/shard_map/all_to_all | solution.py:476
  136.7 26.6 %collective-permute-start.3 = (bf16[128,4096]{1,0:T(8,128)(2,1)}, bf16[128,4096]{1,0:T(8,128)(2,1)S(1)}, u32[]{:S(2)}, u32[]{:S(2)}) collective-permute-start(bf16[128,4096]{1,0:T(8,128)(2,1)} %get-tuple-element.27), channel_id=1, source_target_pairs={{0,3},{1,0},{2,1},{3,2},{4,7},{5,4},{6,5},{7,6},{8,11},{9,8},{10,9... | collective-permute-start | bytes 3145736 | tf_op jit(solution)/shard_map/ppermute | solution.py:470
  138.9 27.8 %collective-permute-start.4 = (bf16[128,4096]{1,0:T(8,128)(2,1)}, bf16[128,4096]{1,0:T(8,128)(2,1)S(1)}, u32[]{:S(2)}, u32[]{:S(2)}) collective-permute-start(bf16[128,4096]{1,0:T(8,128)(2,1)} %get-tuple-element.28), channel_id=1, source_target_pairs={{0,2},{1,3},{2,0},{3,1},{4,6},{5,7},{6,4},{7,5},{8,10},{9,11},{10,... | collective-permute-start | bytes 3145736 | tf_op jit(solution)/shard_map/ppermute | solution.py:470
  143.3 46.9 %collective-permute-start.5 = (bf16[128,4096]{1,0:T(8,128)(2,1)}, bf16[128,4096]{1,0:T(8,128)(2,1)S(1)}, u32[]{:S(2)}, u32[]{:S(2)}) collective-permute-start(bf16[128,4096]{1,0:T(8,128)(2,1)} %get-tuple-element.29), channel_id=1, source_target_pairs={{0,1},{1,2},{2,3},{3,0},{4,5},{5,6},{6,7},{7,4},{8,9},{9,10},{10,1... | collective-permute-start | bytes 3145736 | tf_op jit(solution)/shard_map/ppermute | solution.py:470

commit v4 on v3

--- a/solution.py
+++ b/solution.py
@@ -9,7 +9,7 @@
 MIB = 1024 * 1024
 PARTS = 8
 STEPS = 4
-AHEAD = 4
+AHEAD = 6
 SIZE = 512
 CHUNK = 256
 
@@ -184,7 +184,7 @@
 
 
 def middle_kernel(
-    x_hbm, dy_hbm, xt_hbm, dyt_hbm, rw_hbm, w_hbm, term_ref, act_ref, x, dy, xt, dyt, rw, w, act, ready, pre, sem, flip_sem, out_sem
+    x_hbm, dy_hbm, xt_hbm, dyt_hbm, rw_hbm, w_hbm, term_ref, act_ref, x, dy, xt, dyt, rw, w, act, act_rest, ready, pre, rest, sem, flip_sem, out_sem
 ):
     tok, width = x.shape
 
@@ -216,10 +216,9 @@
             copy.start()
         started += 1
         part = pl.ds(i * depth, depth)
-        for left, cols in ((x, slice(0, 512)), (x, slice(768, 896)), (dy, slice(512, 768)), (dy, slice(768, 896))):
-            to = slice(896, 1024) if left is dy and cols.start == 768 else cols
+        for left, cols in ((x, slice(0, 512)), (dy, slice(512, 768))):
             term = dot(left[:, part], w[part, cols])
-            pre[:, to] = term if i == 0 else pre[:, to] + term
+            pre[:, cols] = term if i == 0 else pre[:, cols] + term
     for group in waiting[started:]:
         for copy in group:
             copy.start()
@@ -236,41 +235,54 @@
     chunk = CHUNK
     lane = lane_index((chunk, LANES))
 
+    def shares(rows):
+        share = rw[rows, :].astype(jnp.float32)
+        return share[:, 0:1], share[:, 1:2], share[:, 2:3]
+
     for i in range(tok // chunk):
         rows = pl.ds(i * chunk, chunk)
-        share = rw[rows, :].astype(jnp.float32)
-        one, two, three = share[:, 0:1], share[:, 1:2], share[:, 2:3]
+        one, two, three = shares(rows)
         for h, part in enumerate((jnp.where(lane < 96, one, two), jnp.where(lane < 64, two, three))):
             at = [slice(256 * m + 128 * h, 256 * m + 128 * h + 128) for m in range(3)]
             for span, value in zip(at, finish(*[pre[rows, span] for span in at], part)):
                 act[rows, span] = value.astype(jnp.bfloat16)
-        tail_x, tail_dy = pre[rows, 768:896], pre[rows, 896:1024]
+    rest[:, 0:128] = dot(x[...], w[:, 768:896])
+    rest[:, 128:256] = dot(dy[...], w[:, 768:896])
+    put_act = [
+        pltpu.make_async_copy(act, act_ref.at[:, pl.ds(0, 768)], sem.at[3 * steps + 1]),
+        pltpu.make_async_copy(act_rest, act_ref.at[:, pl.ds(768, 256)], sem.at[3 * steps + 2]),
+    ]
+    put_act[0].start()
+
+    def send(i):
+        part = pl.ds(pl.multiple_of(i * size, size), size)
+        return pltpu.make_async_copy(ready.at[part], term_ref.at[part], out_sem.at[i])
+
+    for group in waiting[steps + 1 :]:
+        for copy in group:
+            copy.wait()
+    for i in range(tok // chunk):
+        rows = pl.ds(i * chunk, chunk)
+        three = shares(rows)[2]
+        tail_x, tail_dy = rest[rows, 0:128], rest[rows, 128:256]
         d_gate, d_up, weighted = finish(tail_x, pltpu.roll(tail_x, 96, 1), pltpu.roll(tail_dy, 64, 1), three)
         from_x = jnp.where(lane < 32, d_gate, jnp.where(lane < 64, pltpu.roll(d_up, 32, 1), 0.0))
         from_dy = jnp.where((lane >= 64) & (lane < 96), pltpu.roll(weighted, 64, 1), 0.0)
-        act[rows, 768:896] = from_x.astype(jnp.bfloat16)
-        act[rows, 896:1024] = from_dy.astype(jnp.bfloat16)
-
-    put_act = pltpu.make_async_copy(act, act_ref, sem.at[3 * steps + 1])
-    put_act.start()
-
-    def send(i):
-        part = pl.ds(pl.multiple_of(i * size, size), size)
-        return pltpu.make_async_copy(ready.at[part], term_ref.at[part], out_sem.at[i])
-
-    for group in waiting[steps + 1 :]:
-        for copy in group:
-            copy.wait()
+        act_rest[rows, 0:128] = from_x.astype(jnp.bfloat16)
+        act_rest[rows, 128:256] = from_dy.astype(jnp.bfloat16)
     for i in range(width // size):
         cols = pl.ds(i * size, size)
         left, right = xt[cols, :], dyt[cols, :]
         ready[cols, 0:512] = dot(left, act[:, 0:512]).astype(jnp.bfloat16)
         ready[cols, 512:768] = dot(right, act[:, 512:768]).astype(jnp.bfloat16)
-        tail = dot(left, act[:, 768:896]) + dot(right, act[:, 896:1024])
+        tail = dot(left, act_rest[:, 0:128]) + dot(right, act_rest[:, 128:256])
         ready[cols, 768:896] = tail.astype(jnp.bfloat16)
         send(i).start()
-
-    put_act.wait()
+        if i == 0:
+            put_act[1].start()
+
+    for copy in put_act:
+        copy.wait()
     for i in range(width // size):
         send(i).wait()
 
@@ -389,10 +401,12 @@
     tok, width = x.shape
     scratch = (
         *[VMEM(a.shape, jnp.bfloat16) for a in (x, dy, xt, dyt, rw, weights)],
-        VMEM((tok, 1024), jnp.bfloat16),
+        VMEM((tok, 768), jnp.bfloat16),
+        VMEM((tok, 256), jnp.bfloat16),
         VMEM((width, COLUMNS), jnp.bfloat16),
-        VMEM((tok, 1024), jnp.float32),
-        pltpu.SemaphoreType.DMA((3 * STEPS + 2,)),
+        VMEM((tok, 768), jnp.float32),
+        VMEM((tok, 256), jnp.float32),
+        pltpu.SemaphoreType.DMA((3 * STEPS + 3,)),
         pltpu.SemaphoreType.DMA((2 * width // SIZE,)),
         pltpu.SemaphoreType.DMA((width // SIZE,)),
     )

time: 222 us -> 221 us (level)
  the two profiles are of different devices: /device:TPU:29 before, /device:TPU:27 now
where the time goes in v4:
time: 221 us
  waiting for transfers between devices  133 us (60%)
  starting transfers between devices  45.9 us (21%)
  Pallas kernels  37.8 us (17%)
    ppermute x6, waiting for transfers between devices, shift(): lax.ppermute(value, 'narrow', [(i, (i + step) % devices) for i in range(d...  86.9 us
    pallas_call x5, Pallas kernels, call(): pl.pallas_call(body, out_shape=outputs, in_specs=[pl.BlockSpec(memory_spa...  37.8 us
    all_to_all x1, waiting for transfers between devices, per_device(): lax.all_to_all(terms.reshape(groups, owner_rows, COLUMNS), 'wide', split_...  23.5 us
    all_to_all x1, waiting for transfers between devices, per_device(): lax.all_to_all(sent, 'wide', split_axis=0, concat_axis=0, tiled=True)  22.4 us
    ppermute x6, starting transfers between devices, shift(): lax.ppermute(value, 'narrow', [(i, (i + step) % devices) for i in range(d...  19.3 us
    all_to_all x1, starting transfers between devices, per_device(): lax.all_to_all(sent, 'wide', split_axis=0, concat_axis=0, tiled=True)  18.2 us
    all_to_all x1, starting transfers between devices, per_device(): lax.all_to_all(terms.reshape(groups, owner_rows, COLUMNS), 'wide', split_...  8.47 us
  transfers between devices with their start and end apart: 8, of which 8 were waited for; matrix products, arithmetic and copies ran while one was open for 1% of the time, Pallas kernels for 8%

profile of v4, /device:TPU:27, one launch (start us, length us, event | category | flops | bytes accessed | tf_op | source)
XLA Modules:
  0.0 220.7 jit_solution(16650639475167849795)
XLA Ops:
  0.6 4.5 %shard_map.147 = bf16[128,16,896]{2,1,0:T(8,128)(2,1)} custom-call(s32[3,128]{1,0:T(4,128)} %bitcast.4, bf16[16,96,128]{2,1,0:T(8,128)(2,1)} %gate_hbm.1, bf16[16,96,128]{2,1,0:T(8,128)(2,1)} %up_hbm.1, bf16[16,96,128]{2,1,0:T(8,128)(2,1)} %down_hbm.1, bf16[16,128]{1,0:T(8,128)(2,1)} %gs_hbm.1, bf16[16,128]{1,0:T(8,128)(2,1)} %us_hbm.1, bf16[16,128]{1,0:T(8,128)(2,1)} %ds_hbm.1), custom_call_target="tpu_custom_call" | custom-call | bytes 4863488 | tf_op jit(solution)/shard_map/pallas_call | solution.py:340
  5.1 0.0 copy-start.6
  5.1 0.0 copy-start.5
  5.1 0.0 copy-start.3
  5.2 0.0 copy-start.4
  5.2 18.2 %all-to-all-start = ((bf16[128,16,896]{2,1,0:T(8,128)(2,1)}), bf16[128,16,896]{2,1,0:T(8,128)(2,1)}, u32[]{:S(2)}, u32[]{:S(2)}) async-start(bf16[128,16,896]{2,1,0:T(8,128)(2,1)} %shard_map.147), calls=%async_computation | async-start | bytes 7340032 | tf_op jit(solution)/shard_map/all_to_all | solution.py:480
  23.4 0.0 copy-done.6
  23.4 0.0 copy-done.5
  23.4 0.1 select_reduce_fusion
  23.6 0.0 copy-done.3
  23.6 0.0 copy-done.4
  23.6 0.1 pad_maximum_fusion.refs_0_
  23.7 0.0 copy-start
  23.7 2.2 collective-permute-start.2
  25.9 4.0 %collective-permute-start.1 = (bf16[128,4224]{1,0:T(8,128)(2,1)S(1)}, bf16[128,4224]{1,0:T(8,128)(2,1)S(1)}, u32[]{:S(2)}, u32[]{:S(2)}) collective-permute-start(bf16[128,4224]{1,0:T(8,128)(2,1)S(1)} %pad_maximum_fusion.refs_0_), channel_id=1, source_target_pairs={{0,2},{1,3},{2,0},{3,1},{4,6},{5,7},{6,4},{7,5},{8,10},{9,11},{10,... | collective-permute-start | bytes 3244040 | tf_op jit(solution)/shard_map/ppermute | solution.py:484
  29.9 3.4 %collective-permute-start = (bf16[128,4224]{1,0:T(8,128)(2,1)S(1)}, bf16[128,4224]{1,0:T(8,128)(2,1)}, u32[]{:S(2)}, u32[]{:S(2)}) collective-permute-start(bf16[128,4224]{1,0:T(8,128)(2,1)S(1)} %pad_maximum_fusion.refs_0_), channel_id=1, source_target_pairs={{0,1},{1,2},{2,3},{3,0},{4,5},{5,6},{6,7},{7,4},{8,9},{9,10},{10,1... | collective-permute-start | bytes 3244040 | tf_op jit(solution)/shard_map/ppermute | solution.py:484
  33.3 17.4 %collective-permute-done.2.refs_3_ = bf16[128,4224]{1,0:T(8,128)(2,1)S(1)} collective-permute-done((bf16[128,4224]{1,0:T(8,128)(2,1)S(1)}, bf16[128,4224]{1,0:T(8,128)(2,1)S(1)}, u32[]{:S(2)}, u32[]{:S(2)}) %collective-permute-start.2) | collective-permute-done | bytes 1081376 | tf_op jit(solution)/shard_map/ppermute | solution.py:484
  50.8 0.0 copy-start.1
  50.8 24.1 %collective-permute-done.1.refs_2_ = bf16[128,4224]{1,0:T(8,128)(2,1)S(1)} collective-permute-done((bf16[128,4224]{1,0:T(8,128)(2,1)S(1)}, bf16[128,4224]{1,0:T(8,128)(2,1)S(1)}, u32[]{:S(2)}, u32[]{:S(2)}) %collective-permute-start.1) | collective-permute-done | bytes 1081376 | tf_op jit(solution)/shard_map/ppermute | solution.py:484
  74.9 0.0 copy-start.2
  74.9 2.5 %collective-permute-done.refs_1_ = bf16[128,4224]{1,0:T(8,128)(2,1)} collective-permute-done((bf16[128,4224]{1,0:T(8,128)(2,1)S(1)}, bf16[128,4224]{1,0:T(8,128)(2,1)}, u32[]{:S(2)}, u32[]{:S(2)}) %collective-permute-start) | collective-permute-done | bytes 1081376 | tf_op jit(solution)/shard_map/ppermute | solution.py:484
  77.4 0.0 copy-done
  77.4 0.0 copy-done.1
  77.4 0.0 copy-done.2
  77.4 10.2 %shard_map.146 = (s32[3,128]{1,0:T(4,128)}, bf16[512,2048]{1,0:T(8,128)(2,1)}, bf16[512,2048]{1,0:T(8,128)(2,1)}, bf16[2048,512]{1,0:T(8,128)(2,1)}, bf16[2048,5...) custom-call(s32[3,128]{1,0:T(4,128)} %bitcast.5, bf16[128,4224]{1,0:T(8,128)(2,1)} %copy-done, ...), custom_call_target="tpu_custom_call" | custom-call | bytes 12848128 | tf_op jit(solution)/shard_map/pallas_call | solution.py:340
  87.6 22.4 %all-to-all-done = bf16[128,16,896]{2,1,0:T(8,128)(2,1)} async-done(((bf16[128,16,896]{2,1,0:T(8,128)(2,1)}), bf16[128,16,896]{2,1,0:T(8,128)(2,1)}, u32[]{:S(2)}, u32[]{:S(2)}) %all-to-all-start) | async-done | bytes 3670048 | tf_op jit(solution)/shard_map/all_to_all | solution.py:480
  110.0 9.9 %shard_map.148 = (bf16[2048,896]{1,0:T(8,128)(2,1)}, bf16[512,1024]{1,0:T(8,128)(2,1)}) custom-call(bf16[512,2048]{1,0:T(8,128)(2,1)} %get-tuple-element.20.x_hbm, bf16[512,2048]{1,0:T(8,128)(2,1)} %get-tuple-element.21.dy_hbm, bf16[2048,512]{1,0:T(8,128)(2,1)} %get-tuple-element.22.xt_hbm, bf16[2048,512]{1,0:T(8,128)(2,1)} %get-tuple-element.23.dyt_hbm, ...), custom_call_target="tpu_custom_call" | custom-call | flops 3623878656 | bytes 16908288 | tf_op jit(solution)/shard_map/pallas_call | solution.py:340
  119.9 8.5 %all-to-all-start.1 = ((bf16[128,16,896]{2,1,0:T(8,128)(2,1)}), bf16[128,16,896]{2,1,0:T(8,128)(2,1)}, u32[]{:S(2)}, u32[]{:S(2)}) async-start(bf16[128,16,896]{2,1,0:T(8,128)(2,1)} %bitcast.3), calls=%async_computation.1 | async-start | bytes 7340032 | tf_op jit(solution)/shard_map/all_to_all | solution.py:490
  128.4 7.8 %shard_map.149 = (bf16[128,4096]{1,0:T(8,128)(2,1)}, bf16[128,4096]{1,0:T(8,128)(2,1)}, bf16[128,4096]{1,0:T(8,128)(2,1)}, bf16[128,4096]{1,0:T(8,128)(2,1)}) custom-call(bf16[512,1024]{1,0:T(8,128)(2,1)} %get-tuple-element.25.act_ref, bf16[2048,896]{1,0:T(8,128)(2,1)} %bitcast.1.w_hbm.w_ref), custom_call_target="tpu_custom_call" | custom-call | flops 1811939328 | bytes 8912896 | tf_op jit(solution)/shard_map/pallas_call | solution.py:340
  136.1 2.1 collective-permute-start.3
  138.3 4.1 %collective-permute-start.4 = (bf16[128,4096]{1,0:T(8,128)(2,1)}, bf16[128,4096]{1,0:T(8,128)(2,1)S(1)}, u32[]{:S(2)}, u32[]{:S(2)}) collective-permute-start(bf16[128,4096]{1,0:T(8,128)(2,1)} %get-tuple-element.28), channel_id=1, source_target_pairs={{0,2},{1,3},{2,0},{3,1},{4,6},{5,7},{6,4},{7,5},{8,10},{9,11},{10,... | collective-permute-start | bytes 3145736 | tf_op jit(solution)/shard_map/ppermute | solution.py:484
  142.3 3.4 %collective-permute-start.5 = (bf16[128,4096]{1,0:T(8,128)(2,1)}, bf16[128,4096]{1,0:T(8,128)(2,1)S(1)}, u32[]{:S(2)}, u32[]{:S(2)}) collective-permute-start(bf16[128,4096]{1,0:T(8,128)(2,1)} %get-tuple-element.29), channel_id=1, source_target_pairs={{0,1},{1,2},{2,3},{3,0},{4,5},{5,6},{6,7},{7,4},{8,9},{9,10},{10,1... | collective-permute-start | bytes 3145736 | tf_op jit(solution)/shard_map/ppermute | solution.py:484
  145.8 16.9 %collective-permute-done.3 = bf16[128,4096]{1,0:T(8,128)(2,1)S(1)} collective-permute-done((bf16[128,4096]{1,0:T(8,128)(2,1)}, bf16[128,4096]{1,0:T(8,128)(2,1)S(1)}, u32[]{:S(2)}, u32[]{:S(2)}) %collective-permute-start.3) | collective-permute-done | bytes 1048608 | tf_op jit(solution)/shard_map/ppermute | solution.py:484
  162.7 23.4 %collective-permute-done.4 = bf16[128,4096]{1,0:T(8,128)(2,1)S(1)} collective-permute-done((bf16[128,4096]{1,0:T(8,128)(2,1)}, bf16[128,4096]{1,0:T(8,128)(2,1)S(1)}, u32[]{:S(2)}, u32[]{:S(2)}) %collective-permute-start.4) | collective-permute-done | bytes 1048608 | tf_op jit(solution)/shard_map/ppermute | solution.py:484
  186.1 2.5 %collective-permute-done.5 = bf16[128,4096]{1,0:T(8,128)(2,1)S(1)} collective-permute-done((bf16[128,4096]{1,0:T(8,128)(2,1)}, bf16[128,4096]{1,0:T(8,128)(2,1)S(1)}, u32[]{:S(2)}, u32[]{:S(2)}) %collective-permute-start.5) | collective-permute-done | bytes 1048608 | tf_op jit(solution)/shard_map/ppermute | solution.py:484
  188.6 1.9 add_convert_fusion
  190.5 1.0 fusion
  191.5 23.5 %all-to-all-done.1.recv_ref = bf16[128,16,896]{2,1,0:T(8,128)(2,1)} async-done(((bf16[128,16,896]{2,1,0:T(8,128)(2,1)}), bf16[128,16,896]{2,1,0:T(8,128)(2,1)}, u32[]{:S(2)}, u32[]{:S(2)}) %all-to-all-start.1) | async-done | bytes 3670048 | tf_op jit(solution)/shard_map/all_to_all | solution.py:490
  215.0 5.5 %shard_map.150 = (bf16[16,96,128]{2,1,0:T(8,128)(2,1)}, bf16[16,96,128]{2,1,0:T(8,128)(2,1)}, bf16[16,96,128]{2,1,0:T(8,128)(2,1)}) custom-call(s32[3,128]{1,0:T(4,128)} %get-tuple-element.30.places_hbm, bf16[128,16,896]{2,1,0:T(8,128)(2,1)} %all-to-all-done.1.recv_ref), custom_call_target="tpu_custom_call" | custom-call | bytes 4851200 | tf_op jit(solution)/shard_map/pallas_call | solution.py:340
  (2 shorter events, 0.0 us)
Async XLA Ops:
  5.1 18.3 %copy-start.6 = (s32[128,2]{0,1:T(2,128)S(1)}, s32[128,2]{0,1:T(2,128)}, u32[]{:S(2)}) copy-start(s32[128,2]{0,1:T(2,128)} %param.13) | copy-start | bytes 3076
  5.1 18.3 %copy-start.5 = (s32[128,2]{0,1:T(2,128)S(1)}, s32[128,2]{0,1:T(2,128)}, u32[]{:S(2)}) copy-start(s32[128,2]{0,1:T(2,128)} %param.12) | copy-start | bytes 3076
  5.1 18.4 %copy-start.3 = (bf16[128,2048]{1,0:T(8,128)(2,1)S(1)}, bf16[128,2048]{1,0:T(8,128)(2,1)}, u32[]{:S(2)}) copy-start(bf16[128,2048]{1,0:T(8,128)(2,1)} %param.21) | copy-start | bytes 1572868
  5.2 18.4 %copy-start.4 = (bf16[128,2048]{1,0:T(8,128)(2,1)S(1)}, bf16[128,2048]{1,0:T(8,128)(2,1)}, u32[]{:S(2)}) copy-start(bf16[128,2048]{1,0:T(8,128)(2,1)} %param.11) | copy-start | bytes 1572868
  5.2 104.8 %all-to-all-start = ((bf16[128,16,896]{2,1,0:T(8,128)(2,1)}), bf16[128,16,896]{2,1,0:T(8,128)(2,1)}, u32[]{:S(2)}, u32[]{:S(2)}) async-start(bf16[128,16,896]{2,1,0:T(8,128)(2,1)} %shard_map.147), calls=%async_computation | async-start | bytes 7340032 | tf_op jit(solution)/shard_map/all_to_all | solution.py:480
  23.7 53.7 %copy-start = (bf16[128,4224]{1,0:T(8,128)(2,1)}, bf16[128,4224]{1,0:T(8,128)(2,1)S(1)}, u32[]{:S(2)}) copy-start(bf16[128,4224]{1,0:T(8,128)(2,1)S(1)} %pad_maximum_fusion.refs_0_) | copy-start | bytes 3244036
  23.7 27.1 %collective-permute-start.2 = (bf16[128,4224]{1,0:T(8,128)(2,1)S(1)}, bf16[128,4224]{1,0:T(8,128)(2,1)S(1)}, u32[]{:S(2)}, u32[]{:S(2)}) collective-permute-start(bf16[128,4224]{1,0:T(8,128)(2,1)S(1)} %pad_maximum_fusion.refs_0_), channel_id=1, source_target_pairs={{0,3},{1,0},{2,1},{3,2},{4,7},{5,4},{6,5},{7,6},{8,11},{9,8},{10,9... | collective-permute-start | bytes 3244040 | tf_op jit(solution)/shard_map/ppermute | solution.py:484
  25.9 49.0 %collective-permute-start.1 = (bf16[128,4224]{1,0:T(8,128)(2,1)S(1)}, bf16[128,4224]{1,0:T(8,128)(2,1)S(1)}, u32[]{:S(2)}, u32[]{:S(2)}) collective-permute-start(bf16[128,4224]{1,0:T(8,128)(2,1)S(1)} %pad_maximum_fusion.refs_0_), channel_id=1, source_target_pairs={{0,2},{1,3},{2,0},{3,1},{4,6},{5,7},{6,4},{7,5},{8,10},{9,11},{10,... | collective-permute-start | bytes 3244040 | tf_op jit(solution)/shard_map/ppermute | solution.py:484
  29.9 47.5 %collective-permute-start = (bf16[128,4224]{1,0:T(8,128)(2,1)S(1)}, bf16[128,4224]{1,0:T(8,128)(2,1)}, u32[]{:S(2)}, u32[]{:S(2)}) collective-permute-start(bf16[128,4224]{1,0:T(8,128)(2,1)S(1)} %pad_maximum_fusion.refs_0_), channel_id=1, source_target_pairs={{0,1},{1,2},{2,3},{3,0},{4,5},{5,6},{6,7},{7,4},{8,9},{9,10},{10,1... | collective-permute-start | bytes 3244040 | tf_op jit(solution)/shard_map/ppermute | solution.py:484
  50.8 26.6 %copy-start.1 = (bf16[128,4224]{1,0:T(8,128)(2,1)}, bf16[128,4224]{1,0:T(8,128)(2,1)S(1)}, u32[]{:S(2)}) copy-start(bf16[128,4224]{1,0:T(8,128)(2,1)S(1)} %collective-permute-done.2.refs_3_) | copy-start | bytes 3244036
  74.9 2.5 %copy-start.2 = (bf16[128,4224]{1,0:T(8,128)(2,1)}, bf16[128,4224]{1,0:T(8,128)(2,1)S(1)}, u32[]{:S(2)}) copy-start(bf16[128,4224]{1,0:T(8,128)(2,1)S(1)} %collective-permute-done.1.refs_2_) | copy-start | bytes 3244036
  119.9 95.1 %all-to-all-start.1 = ((bf16[128,16,896]{2,1,0:T(8,128)(2,1)}), bf16[128,16,896]{2,1,0:T(8,128)(2,1)}, u32[]{:S(2)}, u32[]{:S(2)}) async-start(bf16[128,16,896]{2,1,0:T(8,128)(2,1)} %bitcast.3), calls=%async_computation.1 | async-start | bytes 7340032 | tf_op jit(solution)/shard_map/all_to_all | solution.py:490
  136.1 26.6 %collective-permute-start.3 = (bf16[128,4096]{1,0:T(8,128)(2,1)}, bf16[128,4096]{1,0:T(8,128)(2,1)S(1)}, u32[]{:S(2)}, u32[]{:S(2)}) collective-permute-start(bf16[128,4096]{1,0:T(8,128)(2,1)} %get-tuple-element.27), channel_id=1, source_target_pairs={{0,3},{1,0},{2,1},{3,2},{4,7},{5,4},{6,5},{7,6},{8,11},{9,8},{10,9... | collective-permute-start | bytes 3145736 | tf_op jit(solution)/shard_map/ppermute | solution.py:484
  138.3 47.8 %collective-permute-start.4 = (bf16[128,4096]{1,0:T(8,128)(2,1)}, bf16[128,4096]{1,0:T(8,128)(2,1)S(1)}, u32[]{:S(2)}, u32[]{:S(2)}) collective-permute-start(bf16[128,4096]{1,0:T(8,128)(2,1)} %get-tuple-element.28), channel_id=1, source_target_pairs={{0,2},{1,3},{2,0},{3,1},{4,6},{5,7},{6,4},{7,5},{8,10},{9,11},{10,... | collective-permute-start | bytes 3145736 | tf_op jit(solution)/shard_map/ppermute | solution.py:484
  142.3 46.3 %collective-permute-start.5 = (bf16[128,4096]{1,0:T(8,128)(2,1)}, bf16[128,4096]{1,0:T(8,128)(2,1)S(1)}, u32[]{:S(2)}, u32[]{:S(2)}) collective-permute-start(bf16[128,4096]{1,0:T(8,128)(2,1)} %get-tuple-element.29), channel_id=1, source_target_pairs={{0,1},{1,2},{2,3},{3,0},{4,5},{5,6},{6,7},{7,4},{8,9},{9,10},{10,1... | collective-permute-start | bytes 3145736 | tf_op jit(solution)/shard_map/ppermute | solution.py:484

commit v5 on v4

--- a/solution.py
+++ b/solution.py
@@ -165,9 +165,9 @@
             grads[m, r] = out[m]
 
     puts = []
-    for half in range(2):
-        part = pl.ds(half * rows // 2, rows // 2)
-        batched(rows // 2, 8, lambda r, h=half: flipped(h * rows // 2 + r), lambda r, out, h=half: finish(h * rows // 2 + r, out))
+    for half in range(4):
+        part = pl.ds(half * rows // 4, rows // 4)
+        batched(rows // 4, 4, lambda r, h=half: flipped(h * rows // 4 + r), lambda r, out, h=half: finish(h * rows // 4 + r, out))
         for m, ref in enumerate((gate_ref, up_ref, down_ref)):
             puts.append(pltpu.make_async_copy(grads.at[m, part], ref.at[part], out_sem.at[3 * half + m]))
             puts[-1].start()
@@ -184,7 +184,7 @@
 
 
 def middle_kernel(
-    x_hbm, dy_hbm, xt_hbm, dyt_hbm, rw_hbm, w_hbm, term_ref, act_ref, x, dy, xt, dyt, rw, w, act, act_rest, ready, pre, rest, sem, flip_sem, out_sem
+    x_hbm, dy_hbm, xt_hbm, dyt_hbm, rw_hbm, w_hbm, term_ref, act_ref, x, dy, flips, rw, w, act, act_rest, ready, pre, rest, sem, flip_sem, out_sem
 ):
     tok, width = x.shape
 
@@ -198,7 +198,7 @@
 
     def flipped(i):
         part = pl.ds(i * size, size)
-        pairs = ((xt_hbm.at[part], xt.at[part]), (dyt_hbm.at[part], dyt.at[part]))
+        pairs = ((xt_hbm.at[part], flips.at[part, pl.ds(0, tok)]), (dyt_hbm.at[part], flips.at[part, pl.ds(tok, tok)]))
         return [pltpu.make_async_copy(*pair, flip_sem.at[2 * i + j]) for j, pair in enumerate(pairs)]
 
     size = SIZE
@@ -250,7 +250,8 @@
     rest[:, 128:256] = dot(dy[...], w[:, 768:896])
     put_act = [
         pltpu.make_async_copy(act, act_ref.at[:, pl.ds(0, 768)], sem.at[3 * steps + 1]),
-        pltpu.make_async_copy(act_rest, act_ref.at[:, pl.ds(768, 256)], sem.at[3 * steps + 2]),
+        pltpu.make_async_copy(act_rest.at[pl.ds(0, tok)], act_ref.at[:, pl.ds(768, 128)], sem.at[3 * steps + 2]),
+        pltpu.make_async_copy(act_rest.at[pl.ds(tok, tok)], act_ref.at[:, pl.ds(896, 128)], sem.at[3 * steps + 3]),
     ]
     put_act[0].start()
 
@@ -268,18 +269,19 @@
         d_gate, d_up, weighted = finish(tail_x, pltpu.roll(tail_x, 96, 1), pltpu.roll(tail_dy, 64, 1), three)
         from_x = jnp.where(lane < 32, d_gate, jnp.where(lane < 64, pltpu.roll(d_up, 32, 1), 0.0))
         from_dy = jnp.where((lane >= 64) & (lane < 96), pltpu.roll(weighted, 64, 1), 0.0)
-        act_rest[rows, 0:128] = from_x.astype(jnp.bfloat16)
-        act_rest[rows, 128:256] = from_dy.astype(jnp.bfloat16)
+        act_rest[rows, :] = from_x.astype(jnp.bfloat16)
+        act_rest[pl.ds(tok + i * chunk, chunk), :] = from_dy.astype(jnp.bfloat16)
     for i in range(width // size):
         cols = pl.ds(i * size, size)
-        left, right = xt[cols, :], dyt[cols, :]
+        left, right = flips[cols, 0:tok], flips[cols, tok : 2 * tok]
         ready[cols, 0:512] = dot(left, act[:, 0:512]).astype(jnp.bfloat16)
         ready[cols, 512:768] = dot(right, act[:, 512:768]).astype(jnp.bfloat16)
-        tail = dot(left, act_rest[:, 0:128]) + dot(right, act_rest[:, 128:256])
+        tail = dot(flips[cols, :], act_rest[...])
         ready[cols, 768:896] = tail.astype(jnp.bfloat16)
         send(i).start()
         if i == 0:
             put_act[1].start()
+            put_act[2].start()
 
     for copy in put_act:
         copy.wait()
@@ -390,7 +392,7 @@
         VMEM((3, *like.shape), jnp.bfloat16),
         pltpu.SemaphoreType.DMA((PARTS,)),
         pltpu.SemaphoreType.DMA,
-        pltpu.SemaphoreType.DMA((6,)),
+        pltpu.SemaphoreType.DMA((12,)),
     )
     return call(
         settle_kernel, [shape(*like.shape)] * 3, (places, received), [ANY] * 2, [ANY] * 3, scratch, limit=60
@@ -400,13 +402,15 @@
 def middle(x, dy, xt, dyt, rw, weights):
     tok, width = x.shape
     scratch = (
-        *[VMEM(a.shape, jnp.bfloat16) for a in (x, dy, xt, dyt, rw, weights)],
+        *[VMEM(a.shape, jnp.bfloat16) for a in (x, dy)],
+        VMEM((width, 2 * tok), jnp.bfloat16),
+        *[VMEM(a.shape, jnp.bfloat16) for a in (rw, weights)],
         VMEM((tok, 768), jnp.bfloat16),
-        VMEM((tok, 256), jnp.bfloat16),
+        VMEM((2 * tok, 128), jnp.bfloat16),
         VMEM((width, COLUMNS), jnp.bfloat16),
         VMEM((tok, 768), jnp.float32),
         VMEM((tok, 256), jnp.float32),
-        pltpu.SemaphoreType.DMA((3 * STEPS + 3,)),
+        pltpu.SemaphoreType.DMA((3 * STEPS + 4,)),
         pltpu.SemaphoreType.DMA((2 * width // SIZE,)),
         pltpu.SemaphoreType.DMA((width // SIZE,)),
     )

time: 221 us -> 221 us (level)
  the two profiles are of different devices: /device:TPU:27 before, /device:TPU:31 now
where the time goes in v5:
time: 221 us
  waiting for transfers between devices  134 us (61%)
  starting transfers between devices  44.5 us (20%)
  Pallas kernels  37.8 us (17%)
    ppermute x6, waiting for transfers between devices, shift(): lax.ppermute(value, 'narrow', [(i, (i + step) % devices) for i in range(d...  88.3 us
    pallas_call x5, Pallas kernels, call(): pl.pallas_call(body, out_shape=outputs, in_specs=[pl.BlockSpec(memory_spa...  37.8 us
    all_to_all x1, waiting for transfers between devices, per_device(): lax.all_to_all(terms.reshape(groups, owner_rows, COLUMNS), 'wide', split_...  23.5 us
    all_to_all x1, waiting for transfers between devices, per_device(): lax.all_to_all(sent, 'wide', split_axis=0, concat_axis=0, tiled=True)  22.4 us
    all_to_all x1, starting transfers between devices, per_device(): lax.all_to_all(sent, 'wide', split_axis=0, concat_axis=0, tiled=True)  18.2 us
    ppermute x6, starting transfers between devices, shift(): lax.ppermute(value, 'narrow', [(i, (i + step) % devices) for i in range(d...  17.8 us
    all_to_all x1, starting transfers between devices, per_device(): lax.all_to_all(terms.reshape(groups, owner_rows, COLUMNS), 'wide', split_...  8.47 us
  transfers between devices with their start and end apart: 8, of which 6 were waited for; matrix products, arithmetic and copies ran while one was open for 1% of the time, Pallas kernels for 8%

profile of v5, /device:TPU:31, one launch (start us, length us, event | category | flops | bytes accessed | tf_op | source)
XLA Modules:
  0.0 220.7 jit_solution(16011841190715854968)
XLA Ops:
  0.6 4.5 %shard_map.147 = bf16[128,16,896]{2,1,0:T(8,128)(2,1)} custom-call(s32[3,128]{1,0:T(4,128)} %bitcast.4, bf16[16,96,128]{2,1,0:T(8,128)(2,1)} %gate_hbm.1, bf16[16,96,128]{2,1,0:T(8,128)(2,1)} %up_hbm.1, bf16[16,96,128]{2,1,0:T(8,128)(2,1)} %down_hbm.1, bf16[16,128]{1,0:T(8,128)(2,1)} %gs_hbm.1, bf16[16,128]{1,0:T(8,128)(2,1)} %us_hbm.1, bf16[16,128]{1,0:T(8,128)(2,1)} %ds_hbm.1), custom_call_target="tpu_custom_call" | custom-call | bytes 4863488 | tf_op jit(solution)/shard_map/pallas_call | solution.py:342
  5.1 0.0 copy-start.6
  5.1 0.0 copy-start.5
  5.1 0.0 copy-start.3
  5.2 0.0 copy-start.4
  5.2 18.2 %all-to-all-start = ((bf16[128,16,896]{2,1,0:T(8,128)(2,1)}), bf16[128,16,896]{2,1,0:T(8,128)(2,1)}, u32[]{:S(2)}, u32[]{:S(2)}) async-start(bf16[128,16,896]{2,1,0:T(8,128)(2,1)} %shard_map.147), calls=%async_computation | async-start | bytes 7340032 | tf_op jit(solution)/shard_map/all_to_all | solution.py:484
  23.4 0.0 copy-done.6
  23.4 0.0 copy-done.5
  23.4 0.1 select_reduce_fusion
  23.6 0.0 copy-done.3
  23.6 0.0 copy-done.4
  23.6 0.1 pad_maximum_fusion.refs_0_
  23.7 0.0 copy-start
  23.7 2.5 %collective-permute-start.2 = (bf16[128,4224]{1,0:T(8,128)(2,1)S(1)}, bf16[128,4224]{1,0:T(8,128)(2,1)S(1)}, u32[]{:S(2)}, u32[]{:S(2)}) collective-permute-start(bf16[128,4224]{1,0:T(8,128)(2,1)S(1)} %pad_maximum_fusion.refs_0_), channel_id=1, source_target_pairs={{0,3},{1,0},{2,1},{3,2},{4,7},{5,4},{6,5},{7,6},{8,11},{9,8},{10,9... | collective-permute-start | bytes 3244040 | tf_op jit(solution)/shard_map/ppermute | solution.py:488
  26.1 2.7 %collective-permute-start.1 = (bf16[128,4224]{1,0:T(8,128)(2,1)S(1)}, bf16[128,4224]{1,0:T(8,128)(2,1)S(1)}, u32[]{:S(2)}, u32[]{:S(2)}) collective-permute-start(bf16[128,4224]{1,0:T(8,128)(2,1)S(1)} %pad_maximum_fusion.refs_0_), channel_id=1, source_target_pairs={{0,2},{1,3},{2,0},{3,1},{4,6},{5,7},{6,4},{7,5},{8,10},{9,11},{10,... | collective-permute-start | bytes 3244040 | tf_op jit(solution)/shard_map/ppermute | solution.py:488
  28.9 3.7 %collective-permute-start = (bf16[128,4224]{1,0:T(8,128)(2,1)S(1)}, bf16[128,4224]{1,0:T(8,128)(2,1)}, u32[]{:S(2)}, u32[]{:S(2)}) collective-permute-start(bf16[128,4224]{1,0:T(8,128)(2,1)S(1)} %pad_maximum_fusion.refs_0_), channel_id=1, source_target_pairs={{0,1},{1,2},{2,3},{3,0},{4,5},{5,6},{6,7},{7,4},{8,9},{9,10},{10,1... | collective-permute-start | bytes 3244040 | tf_op jit(solution)/shard_map/ppermute | solution.py:488
  32.6 42.5 %collective-permute-done.2.refs_3_ = bf16[128,4224]{1,0:T(8,128)(2,1)S(1)} collective-permute-done((bf16[128,4224]{1,0:T(8,128)(2,1)S(1)}, bf16[128,4224]{1,0:T(8,128)(2,1)S(1)}, u32[]{:S(2)}, u32[]{:S(2)}) %collective-permute-start.2) | collective-permute-done | bytes 1081376 | tf_op jit(solution)/shard_map/ppermute | solution.py:488
  75.2 0.0 copy-start.1
  75.2 0.0 collective-permute-done.1.refs_2_
  75.2 0.0 copy-start.2
  75.2 2.2 %collective-permute-done.refs_1_ = bf16[128,4224]{1,0:T(8,128)(2,1)} collective-permute-done((bf16[128,4224]{1,0:T(8,128)(2,1)S(1)}, bf16[128,4224]{1,0:T(8,128)(2,1)}, u32[]{:S(2)}, u32[]{:S(2)}) %collective-permute-start) | collective-permute-done | bytes 1081376 | tf_op jit(solution)/shard_map/ppermute | solution.py:488
  77.4 0.0 copy-done
  77.4 0.0 copy-done.1
  77.4 0.0 copy-done.2
  77.4 10.2 %shard_map.146 = (s32[3,128]{1,0:T(4,128)}, bf16[512,2048]{1,0:T(8,128)(2,1)}, bf16[512,2048]{1,0:T(8,128)(2,1)}, bf16[2048,512]{1,0:T(8,128)(2,1)}, bf16[2048,5...) custom-call(s32[3,128]{1,0:T(4,128)} %bitcast.5, bf16[128,4224]{1,0:T(8,128)(2,1)} %copy-done, ...), custom_call_target="tpu_custom_call" | custom-call | bytes 12848128 | tf_op jit(solution)/shard_map/pallas_call | solution.py:342
  87.6 22.4 %all-to-all-done = bf16[128,16,896]{2,1,0:T(8,128)(2,1)} async-done(((bf16[128,16,896]{2,1,0:T(8,128)(2,1)}), bf16[128,16,896]{2,1,0:T(8,128)(2,1)}, u32[]{:S(2)}, u32[]{:S(2)}) %all-to-all-start) | async-done | bytes 3670048 | tf_op jit(solution)/shard_map/all_to_all | solution.py:484
  110.0 9.9 %shard_map.148 = (bf16[2048,896]{1,0:T(8,128)(2,1)}, bf16[512,1024]{1,0:T(8,128)(2,1)}) custom-call(bf16[512,2048]{1,0:T(8,128)(2,1)} %get-tuple-element.20.x_hbm, bf16[512,2048]{1,0:T(8,128)(2,1)} %get-tuple-element.21.dy_hbm, bf16[2048,512]{1,0:T(8,128)(2,1)} %get-tuple-element.22.xt_hbm, bf16[2048,512]{1,0:T(8,128)(2,1)} %get-tuple-element.23.dyt_hbm, ...), custom_call_target="tpu_custom_call" | custom-call | flops 3623878656 | bytes 16908288 | tf_op jit(solution)/shard_map/pallas_call | solution.py:342
  119.9 8.5 %all-to-all-start.1 = ((bf16[128,16,896]{2,1,0:T(8,128)(2,1)}), bf16[128,16,896]{2,1,0:T(8,128)(2,1)}, u32[]{:S(2)}, u32[]{:S(2)}) async-start(bf16[128,16,896]{2,1,0:T(8,128)(2,1)} %bitcast.3), calls=%async_computation.1 | async-start | bytes 7340032 | tf_op jit(solution)/shard_map/all_to_all | solution.py:494
  128.4 7.7 %shard_map.149 = (bf16[128,4096]{1,0:T(8,128)(2,1)}, bf16[128,4096]{1,0:T(8,128)(2,1)}, bf16[128,4096]{1,0:T(8,128)(2,1)}, bf16[128,4096]{1,0:T(8,128)(2,1)}) custom-call(bf16[512,1024]{1,0:T(8,128)(2,1)} %get-tuple-element.25.act_ref, bf16[2048,896]{1,0:T(8,128)(2,1)} %bitcast.1.w_hbm.w_ref), custom_call_target="tpu_custom_call" | custom-call | flops 1811939328 | bytes 8912896 | tf_op jit(solution)/shard_map/pallas_call | solution.py:342
  136.1 2.4 %collective-permute-start.3 = (bf16[128,4096]{1,0:T(8,128)(2,1)}, bf16[128,4096]{1,0:T(8,128)(2,1)S(1)}, u32[]{:S(2)}, u32[]{:S(2)}) collective-permute-start(bf16[128,4096]{1,0:T(8,128)(2,1)} %get-tuple-element.27), channel_id=1, source_target_pairs={{0,3},{1,0},{2,1},{3,2},{4,7},{5,4},{6,5},{7,6},{8,11},{9,8},{10,9... | collective-permute-start | bytes 3145736 | tf_op jit(solution)/shard_map/ppermute | solution.py:488
  138.6 2.7 %collective-permute-start.4 = (bf16[128,4096]{1,0:T(8,128)(2,1)}, bf16[128,4096]{1,0:T(8,128)(2,1)S(1)}, u32[]{:S(2)}, u32[]{:S(2)}) collective-permute-start(bf16[128,4096]{1,0:T(8,128)(2,1)} %get-tuple-element.28), channel_id=1, source_target_pairs={{0,2},{1,3},{2,0},{3,1},{4,6},{5,7},{6,4},{7,5},{8,10},{9,11},{10,... | collective-permute-start | bytes 3145736 | tf_op jit(solution)/shard_map/ppermute | solution.py:488
  141.3 3.7 %collective-permute-start.5 = (bf16[128,4096]{1,0:T(8,128)(2,1)}, bf16[128,4096]{1,0:T(8,128)(2,1)S(1)}, u32[]{:S(2)}, u32[]{:S(2)}) collective-permute-start(bf16[128,4096]{1,0:T(8,128)(2,1)} %get-tuple-element.29), channel_id=1, source_target_pairs={{0,1},{1,2},{2,3},{3,0},{4,5},{5,6},{6,7},{7,4},{8,9},{9,10},{10,1... | collective-permute-start | bytes 3145736 | tf_op jit(solution)/shard_map/ppermute | solution.py:488
  145.1 41.3 %collective-permute-done.3 = bf16[128,4096]{1,0:T(8,128)(2,1)S(1)} collective-permute-done((bf16[128,4096]{1,0:T(8,128)(2,1)}, bf16[128,4096]{1,0:T(8,128)(2,1)S(1)}, u32[]{:S(2)}, u32[]{:S(2)}) %collective-permute-start.3) | collective-permute-done | bytes 1048608 | tf_op jit(solution)/shard_map/ppermute | solution.py:488
  186.4 0.0 collective-permute-done.4
  186.4 2.2 %collective-permute-done.5 = bf16[128,4096]{1,0:T(8,128)(2,1)S(1)} collective-permute-done((bf16[128,4096]{1,0:T(8,128)(2,1)}, bf16[128,4096]{1,0:T(8,128)(2,1)S(1)}, u32[]{:S(2)}, u32[]{:S(2)}) %collective-permute-start.5) | collective-permute-done | bytes 1048608 | tf_op jit(solution)/shard_map/ppermute | solution.py:488
  188.6 1.9 add_convert_fusion
  190.5 1.0 fusion
  191.5 23.5 %all-to-all-done.1.recv_ref = bf16[128,16,896]{2,1,0:T(8,128)(2,1)} async-done(((bf16[128,16,896]{2,1,0:T(8,128)(2,1)}), bf16[128,16,896]{2,1,0:T(8,128)(2,1)}, u32[]{:S(2)}, u32[]{:S(2)}) %all-to-all-start.1) | async-done | bytes 3670048 | tf_op jit(solution)/shard_map/all_to_all | solution.py:494
  215.0 5.5 %shard_map.150 = (bf16[16,96,128]{2,1,0:T(8,128)(2,1)}, bf16[16,96,128]{2,1,0:T(8,128)(2,1)}, bf16[16,96,128]{2,1,0:T(8,128)(2,1)}) custom-call(s32[3,128]{1,0:T(4,128)} %get-tuple-element.30.places_hbm, bf16[128,16,896]{2,1,0:T(8,128)(2,1)} %all-to-all-done.1.recv_ref), custom_call_target="tpu_custom_call" | custom-call | bytes 4851200 | tf_op jit(solution)/shard_map/pallas_call | solution.py:342
  (2 shorter events, 0.0 us)
Async XLA Ops:
  5.1 18.3 %copy-start.6 = (s32[128,2]{0,1:T(2,128)S(1)}, s32[128,2]{0,1:T(2,128)}, u32[]{:S(2)}) copy-start(s32[128,2]{0,1:T(2,128)} %param.13) | copy-start | bytes 3076
  5.1 18.3 %copy-start.5 = (s32[128,2]{0,1:T(2,128)S(1)}, s32[128,2]{0,1:T(2,128)}, u32[]{:S(2)}) copy-start(s32[128,2]{0,1:T(2,128)} %param.12) | copy-start | bytes 3076
  5.1 18.4 %copy-start.3 = (bf16[128,2048]{1,0:T(8,128)(2,1)S(1)}, bf16[128,2048]{1,0:T(8,128)(2,1)}, u32[]{:S(2)}) copy-start(bf16[128,2048]{1,0:T(8,128)(2,1)} %param.21) | copy-start | bytes 1572868
  5.2 18.4 %copy-start.4 = (bf16[128,2048]{1,0:T(8,128)(2,1)S(1)}, bf16[128,2048]{1,0:T(8,128)(2,1)}, u32[]{:S(2)}) copy-start(bf16[128,2048]{1,0:T(8,128)(2,1)} %param.11) | copy-start | bytes 1572868
  5.2 104.8 %all-to-all-start = ((bf16[128,16,896]{2,1,0:T(8,128)(2,1)}), bf16[128,16,896]{2,1,0:T(8,128)(2,1)}, u32[]{:S(2)}, u32[]{:S(2)}) async-start(bf16[128,16,896]{2,1,0:T(8,128)(2,1)} %shard_map.147), calls=%async_computation | async-start | bytes 7340032 | tf_op jit(solution)/shard_map/all_to_all | solution.py:484
  23.7 53.7 %copy-start = (bf16[128,4224]{1,0:T(8,128)(2,1)}, bf16[128,4224]{1,0:T(8,128)(2,1)S(1)}, u32[]{:S(2)}) copy-start(bf16[128,4224]{1,0:T(8,128)(2,1)S(1)} %pad_maximum_fusion.refs_0_) | copy-start | bytes 3244036
  23.7 51.5 %collective-permute-start.2 = (bf16[128,4224]{1,0:T(8,128)(2,1)S(1)}, bf16[128,4224]{1,0:T(8,128)(2,1)S(1)}, u32[]{:S(2)}, u32[]{:S(2)}) collective-permute-start(bf16[128,4224]{1,0:T(8,128)(2,1)S(1)} %pad_maximum_fusion.refs_0_), channel_id=1, source_target_pairs={{0,3},{1,0},{2,1},{3,2},{4,7},{5,4},{6,5},{7,6},{8,11},{9,8},{10,9... | collective-permute-start | bytes 3244040 | tf_op jit(solution)/shard_map/ppermute | solution.py:488
  26.1 49.0 %collective-permute-start.1 = (bf16[128,4224]{1,0:T(8,128)(2,1)S(1)}, bf16[128,4224]{1,0:T(8,128)(2,1)S(1)}, u32[]{:S(2)}, u32[]{:S(2)}) collective-permute-start(bf16[128,4224]{1,0:T(8,128)(2,1)S(1)} %pad_maximum_fusion.refs_0_), channel_id=1, source_target_pairs={{0,2},{1,3},{2,0},{3,1},{4,6},{5,7},{6,4},{7,5},{8,10},{9,11},{10,... | collective-permute-start | bytes 3244040 | tf_op jit(solution)/shard_map/ppermute | solution.py:488
  28.9 48.5 %collective-permute-start = (bf16[128,4224]{1,0:T(8,128)(2,1)S(1)}, bf16[128,4224]{1,0:T(8,128)(2,1)}, u32[]{:S(2)}, u32[]{:S(2)}) collective-permute-start(bf16[128,4224]{1,0:T(8,128)(2,1)S(1)} %pad_maximum_fusion.refs_0_), channel_id=1, source_target_pairs={{0,1},{1,2},{2,3},{3,0},{4,5},{5,6},{6,7},{7,4},{8,9},{9,10},{10,1... | collective-permute-start | bytes 3244040 | tf_op jit(solution)/shard_map/ppermute | solution.py:488
  75.2 2.2 %copy-start.1 = (bf16[128,4224]{1,0:T(8,128)(2,1)}, bf16[128,4224]{1,0:T(8,128)(2,1)S(1)}, u32[]{:S(2)}) copy-start(bf16[128,4224]{1,0:T(8,128)(2,1)S(1)} %collective-permute-done.2.refs_3_) | copy-start | bytes 3244036
  75.2 2.2 %copy-start.2 = (bf16[128,4224]{1,0:T(8,128)(2,1)}, bf16[128,4224]{1,0:T(8,128)(2,1)S(1)}, u32[]{:S(2)}) copy-start(bf16[128,4224]{1,0:T(8,128)(2,1)S(1)} %collective-permute-done.1.refs_2_) | copy-start | bytes 3244036
  119.9 95.1 %all-to-all-start.1 = ((bf16[128,16,896]{2,1,0:T(8,128)(2,1)}), bf16[128,16,896]{2,1,0:T(8,128)(2,1)}, u32[]{:S(2)}, u32[]{:S(2)}) async-start(bf16[128,16,896]{2,1,0:T(8,128)(2,1)} %bitcast.3), calls=%async_computation.1 | async-start | bytes 7340032 | tf_op jit(solution)/shard_map/all_to_all | solution.py:494
  136.1 50.3 %collective-permute-start.3 = (bf16[128,4096]{1,0:T(8,128)(2,1)}, bf16[128,4096]{1,0:T(8,128)(2,1)S(1)}, u32[]{:S(2)}, u32[]{:S(2)}) collective-permute-start(bf16[128,4096]{1,0:T(8,128)(2,1)} %get-tuple-element.27), channel_id=1, source_target_pairs={{0,3},{1,0},{2,1},{3,2},{4,7},{5,4},{6,5},{7,6},{8,11},{9,8},{10,9... | collective-permute-start | bytes 3145736 | tf_op jit(solution)/shard_map/ppermute | solution.py:488
  138.6 47.8 %collective-permute-start.4 = (bf16[128,4096]{1,0:T(8,128)(2,1)}, bf16[128,4096]{1,0:T(8,128)(2,1)S(1)}, u32[]{:S(2)}, u32[]{:S(2)}) collective-permute-start(bf16[128,4096]{1,0:T(8,128)(2,1)} %get-tuple-element.28), channel_id=1, source_target_pairs={{0,2},{1,3},{2,0},{3,1},{4,6},{5,7},{6,4},{7,5},{8,10},{9,11},{10,... | collective-permute-start | bytes 3145736 | tf_op jit(solution)/shard_map/ppermute | solution.py:488
  141.3 47.3 %collective-permute-start.5 = (bf16[128,4096]{1,0:T(8,128)(2,1)}, bf16[128,4096]{1,0:T(8,128)(2,1)S(1)}, u32[]{:S(2)}, u32[]{:S(2)}) collective-permute-start(bf16[128,4096]{1,0:T(8,128)(2,1)} %get-tuple-element.29), channel_id=1, source_target_pairs={{0,1},{1,2},{2,3},{3,0},{4,5},{5,6},{6,7},{7,4},{8,9},{9,10},{10,1... | collective-permute-start | bytes 3145736 | tf_op jit(solution)/shard_map/ppermute | solution.py:488
